TPU v7x, 128 devices: a whole 4x4x4 slice. The times are simulated.
128 devices in a mesh: region: 8 (over z, core), sub: 16 (over y, x).
Axes of the slice: x: 4, y: 4, z: 4, core: 2. Of those that a mesh axis runs over, the one named last changes fastest.
Arguments:
- features: bfloat16 [96, 1048576], P(None, ('region', 'sub')), may hold values from -60 to 60
- neighbors: int32 [27, 1048576], P(None, ('region', 'sub')), may hold values from 0 to 24576, as said below
- send_rows: int32 [128, 16384], P(('region', 'sub')), may hold values from 0 to 8191, as said below
- active_rows: int32 [128], replicated, may hold values from 2048 to 8192, as said below
- weight_one: bfloat16 [27, 96, 96], replicated, may hold values from -0.125 to 0.125
- weight_two: bfloat16 [27, 96, 96], replicated, may hold values from -0.125 to 0.125
- norm_gain: float32 [2, 96], replicated, may hold values from 0.5 to 2
- norm_shift: float32 [2, 96], replicated, may hold values from -1 to 1
Outputs:
- refined: bfloat16 [96, 1048576], P(None, ('region', 'sub'))
Inputs may be any that keep to these rules, and one draw needn't show every extreme that they name: `active_rows`: each entry is a multiple of 128; the busiest device has all 8192 slots occupied; occupied slots come first. `send_rows`: row s lists in slots r * 128 to r * 128 + 127 the local columns of device s, below active_rows[s], whose features device r needs; any device r other than s may receive; the slots that carry voxels come first in each group of 128; a slot that carries nothing holds 0; in every draw some device receives all 128 slots from every other device. `neighbors`: an entry is a local column below the device's active count, an arrived column 8192 + p * 128 + c whose slot carries a voxel, or 24576 for a missing voxel; the middle offset of an active column names the column itself; inactive columns name no voxel; every slot that carries a voxel is named somewhere.
All inputs are finite; a program needn't handle non-finite values.
Results may differ from a plain program's by a relative error of at most 0.0052.
Values may be sent and summed in bfloat16 or wider, within the bound.
No kernel may reach another device: no remote copies, remote signals or barrier semaphores. Data moves between devices by JAX's collectives and lax.ppermute only.
A program may use at most 128 MiB of HBM per device.

v0:
```python
import jax
import jax.numpy as jnp
from jax import lax
from jax.sharding import PartitionSpec as P

BLOCK = 128


NORM_EPS = 1e-05


def convolve(extended, kernel_map, weight):
    extent = kernel_map.shape[1]
    channels = extended.shape[0]
    table = jnp.concatenate(
        [jnp.transpose(extended), jnp.zeros((1, channels), extended.dtype)], axis=0
    )
    pieces = extent // BLOCK
    group = max((g for g in range(1, 17) if pieces % g == 0))
    stride = group * BLOCK
    result = jnp.zeros((weight.shape[2], extent), jnp.float32)

    def advance(turn, current):
        columns = lax.dynamic_slice_in_dim(kernel_map, turn * stride, stride, 1)
        gathered = jnp.take(table, columns, axis=0, mode="clip")
        product = jnp.einsum("kbi,kio->ob", gathered, weight, preferred_element_type=jnp.float32)
        return lax.dynamic_update_slice_in_dim(current, product, turn * stride, 1)

    return lax.fori_loop(0, pieces // group, advance, result)


def route(hidden, outgoing):
    parcel = jnp.transpose(jnp.take(jnp.transpose(hidden), outgoing, axis=0))
    return lax.all_to_all(parcel, ("region", "sub"), split_axis=1, concat_axis=1, tiled=True)


def normalize(conved, active, population, gain, shift):
    masked = jnp.where(active, conved, 0.0)
    average = lax.psum(jnp.sum(masked, axis=1), ("region", "sub")) / population
    offset = jnp.where(active, conved - average[:, None], 0.0)
    spread = lax.psum(jnp.sum(offset * offset, axis=1), ("region", "sub")) / population
    factor = gain * lax.rsqrt(spread + NORM_EPS)
    normed = (conved - average[:, None]) * factor[:, None] + shift[:, None]
    return jnp.where(active, jnp.maximum(normed, 0.0), 0.0).astype(jnp.bfloat16)


def body(
    features, neighbors, send_rows, active_rows, weight_one, weight_two, norm_gain, norm_shift
):
    device = lax.axis_index(("region", "sub"))
    extent = features.shape[1]
    live_count = lax.dynamic_index_in_dim(active_rows, device, keepdims=False)
    active = (jnp.arange(extent, dtype=jnp.int32) < live_count)[None, :]
    population = jnp.sum(active_rows).astype(jnp.float32)
    outgoing = send_rows[0]
    hidden = features
    for depth, weight in enumerate((weight_one, weight_two)):
        arrived = route(hidden, outgoing)
        extended = jnp.concatenate([hidden, arrived], axis=1)
        conved = convolve(extended, neighbors, weight)
        hidden = normalize(conved, active, population, norm_gain[depth], norm_shift[depth])
    return hidden


def solution(mesh):
    placed = (
        P(None, ("region", "sub")),
        P(None, ("region", "sub")),
        P(("region", "sub"), None),
        P(),
        P(),
        P(),
        P(),
        P(),
    )
    return jax.shard_map(
        body, mesh=mesh, in_specs=placed, out_specs=P(None, ("region", "sub")), check_vma=False
    )
```

profile of v0, /device:TPU:1, one launch (start us, length us, event | category | flops | bytes accessed | tf_op | source)
XLA Modules:
  0.0 2153.5 jit_solution(17995170416544863157)
XLA Ops:
  4.9 57.4 %gather_fusion.2 = bf16[16384,96]{1,0:T(8,128)(2,1)} fusion(bf16[8192,96]{1,0:T(8,128)(2,1)S(1)} %bitcast.69, s32[16384]{0:T(1024)S(1)} %fusion.2), kind=kCustom, calls=%fused_computation.clone | custom fusion | bytes 6356992 | tf_op jit(solution)/shard_map/jit(_take)/gather | solution.py:33
  62.3 11.5 broadcast_select_fusion.1
  79.8 11.5 all-to-all-start
  97.1 35.0 %all-to-all-done = bf16[96,128,128]{2,0,1:T(8,128)(2,1)S(1)} async-done(((bf16[96,128,128]{2,0,1:T(8,128)(2,1)}), bf16[96,128,128]{2,0,1:T(8,128)(2,1)S(1)}, u32[]{:S(2)}, u32[]{:S(2)}) %all-to-all-start) | async-done | bytes 3145760 | tf_op jit(solution)/shard_map/all_to_all | solution.py:34
  136.1 8.0 copy.70
  144.1 6.3 concatenate.13.clone
  150.6 799.9 %while.26 = (s32[]{:T(128)}, f32[96,8192]{1,0:T(8,128)S(1)}, s32[27,8192]{1,0:T(8,128)}, bf16[24577,96]{1,0:T(8,128)(2,1)}, bf16[27,96,96]{1,2,0:T(8,128)(2,1)},...) while((s32[]{:T(128)}, f32[96,8192]{1,0:T(8,128)S(1)}, s32[27,8192]{1,0:T(8,128)}, ...), condition=%wide.region_1.3_spmd, body=%wide.region_0.0_spmd.sunk | while | flops 1019271168 | bytes 34683024 | solution.py:29
  153.3 187.9 %gather_fusion = bf16[55296,96]{1,0:T(8,128)(2,1)} fusion(bf16[24577,96]{1,0:T(8,128)(2,1)} %get-tuple-element.341, s32[55296]{0:T(1024)S(1)} %broadcast_clamp_fusion.4), kind=kCustom, calls=%fused_computation.1.clone.1 | custom fusion | bytes 21454848 | tf_op jit(solution)/shard_map/while/body/eval_jaxpr/jit(_take)/gather | solution.py:25
  341.2 9.5 fusion.18
  353.4 187.8 %gather_fusion = bf16[55296,96]{1,0:T(8,128)(2,1)} fusion(bf16[24577,96]{1,0:T(8,128)(2,1)} %get-tuple-element.341, s32[55296]{0:T(1024)S(1)} %broadcast_clamp_fusion.4), kind=kCustom, calls=%fused_computation.1.clone.1 | custom fusion | bytes 21454848 | tf_op jit(solution)/shard_map/while/body/eval_jaxpr/jit(_take)/gather | solution.py:25
  541.1 9.5 fusion.18
  553.3 187.8 %gather_fusion = bf16[55296,96]{1,0:T(8,128)(2,1)} fusion(bf16[24577,96]{1,0:T(8,128)(2,1)} %get-tuple-element.341, s32[55296]{0:T(1024)S(1)} %broadcast_clamp_fusion.4), kind=kCustom, calls=%fused_computation.1.clone.1 | custom fusion | bytes 21454848 | tf_op jit(solution)/shard_map/while/body/eval_jaxpr/jit(_take)/gather | solution.py:25
  741.1 9.5 fusion.18
  753.3 187.8 %gather_fusion = bf16[55296,96]{1,0:T(8,128)(2,1)} fusion(bf16[24577,96]{1,0:T(8,128)(2,1)} %get-tuple-element.341, s32[55296]{0:T(1024)S(1)} %broadcast_clamp_fusion.4), kind=kCustom, calls=%fused_computation.1.clone.1 | custom fusion | bytes 21454848 | tf_op jit(solution)/shard_map/while/body/eval_jaxpr/jit(_take)/gather | solution.py:25
  941.0 9.5 fusion.18
  950.9 64.2 %psum.28 = f32[96]{0:T(128)S(1)} all-reduce(f32[96]{0:T(128)S(1)} %select_reduce_fusion.1), channel_id=1, replica_groups=mesh['region'=8,'sub'=16] {'region','sub'}, use_global_device_ids=true, to_apply=%region_3.5 | all-reduce | flops 96 | bytes 768 | tf_op jit(solution)/shard_map/psum | solution.py:39
  1015.8 62.7 %psum.29 = f32[96]{0:T(128)S(1)} all-reduce(f32[96]{0:T(128)S(1)} %multiply_reduce_fusion.1), channel_id=1, replica_groups=mesh['region'=8,'sub'=16] {'region','sub'}, use_global_device_ids=true, to_apply=%region_6.8 | all-reduce | flops 96 | bytes 768 | tf_op jit(solution)/shard_map/psum | solution.py:41
  1083.5 57.4 %gather_fusion.3 = bf16[16384,96]{1,0:T(8,128)(2,1)} fusion(bf16[8192,96]{1,0:T(8,128)(2,1)S(1)} %copy.63, s32[16384]{0:T(1024)S(1)} %copy-done.5), kind=kCustom, calls=%fused_computation.3.clone | custom fusion | bytes 6356992 | tf_op jit(solution)/shard_map/jit(_take)/gather | solution.py:33
  1140.9 11.5 broadcast_select_fusion
  1168.1 36.6 %all-to-all-done.1 = bf16[96,128,128]{2,0,1:T(8,128)(2,1)} async-done(((bf16[96,128,128]{2,0,1:T(8,128)(2,1)}), bf16[96,128,128]{2,0,1:T(8,128)(2,1)}, u32[]{:S(2)}, u32[]{:S(2)}) %all-to-all-start.1) | async-done | bytes 3145760 | tf_op jit(solution)/shard_map/all_to_all | solution.py:34
  1209.4 8.0 copy.71
  1223.9 799.9 %while.27 = (s32[]{:T(128)}, f32[96,8192]{1,0:T(8,128)S(1)}, s32[27,8192]{1,0:T(8,128)}, bf16[24577,96]{1,0:T(8,128)(2,1)}, bf16[27,96,96]{1,2,0:T(8,128)(2,1)},...) while((s32[]{:T(128)}, f32[96,8192]{1,0:T(8,128)S(1)}, s32[27,8192]{1,0:T(8,128)}, ...), condition=%wide.region_8.10_spmd, body=%wide.region_7.9_spmd.sunk | while | flops 1019271168 | bytes 34683024 | solution.py:29
  1226.6 187.9 %gather_fusion.1 = bf16[55296,96]{1,0:T(8,128)(2,1)} fusion(bf16[24577,96]{1,0:T(8,128)(2,1)} %get-tuple-element.368, s32[55296]{0:T(1024)S(1)} %broadcast_clamp_fusion.5), kind=kCustom, calls=%fused_computation.2.clone.1 | custom fusion | bytes 21454848 | tf_op jit(solution)/shard_map/while/body/eval_jaxpr/jit(_take)/gather | solution.py:25
  1414.5 9.5 fusion.21
  1426.7 187.8 %gather_fusion.1 = bf16[55296,96]{1,0:T(8,128)(2,1)} fusion(bf16[24577,96]{1,0:T(8,128)(2,1)} %get-tuple-element.368, s32[55296]{0:T(1024)S(1)} %broadcast_clamp_fusion.5), kind=kCustom, calls=%fused_computation.2.clone.1 | custom fusion | bytes 21454848 | tf_op jit(solution)/shard_map/while/body/eval_jaxpr/jit(_take)/gather | solution.py:25
  1614.4 9.5 fusion.21
  1626.6 187.8 %gather_fusion.1 = bf16[55296,96]{1,0:T(8,128)(2,1)} fusion(bf16[24577,96]{1,0:T(8,128)(2,1)} %get-tuple-element.368, s32[55296]{0:T(1024)S(1)} %broadcast_clamp_fusion.5), kind=kCustom, calls=%fused_computation.2.clone.1 | custom fusion | bytes 21454848 | tf_op jit(solution)/shard_map/while/body/eval_jaxpr/jit(_take)/gather | solution.py:25
  1814.4 9.5 fusion.21
  1826.6 187.8 %gather_fusion.1 = bf16[55296,96]{1,0:T(8,128)(2,1)} fusion(bf16[24577,96]{1,0:T(8,128)(2,1)} %get-tuple-element.368, s32[55296]{0:T(1024)S(1)} %broadcast_clamp_fusion.5), kind=kCustom, calls=%fused_computation.2.clone.1 | custom fusion | bytes 21454848 | tf_op jit(solution)/shard_map/while/body/eval_jaxpr/jit(_take)/gather | solution.py:25
  2014.3 9.5 fusion.21
  2024.2 64.2 %psum.30 = f32[96]{0:T(128)S(1)} all-reduce(f32[96]{0:T(128)S(1)} %select_reduce_fusion), channel_id=1, replica_groups=mesh['region'=8,'sub'=16] {'region','sub'}, use_global_device_ids=true, to_apply=%region_10.12 | all-reduce | flops 96 | bytes 768 | tf_op jit(solution)/shard_map/psum | solution.py:39
  2089.1 62.6 %psum.31 = f32[96]{0:T(128)S(1)} all-reduce(f32[96]{0:T(128)S(1)} %multiply_reduce_fusion), channel_id=1, replica_groups=mesh['region'=8,'sub'=16] {'region','sub'}, use_global_device_ids=true, to_apply=%region_12.14 | all-reduce | flops 96 | bytes 768 | tf_op jit(solution)/shard_map/psum | solution.py:41
  (87 shorter events, 77.1 us)
Async XLA Ops:
  0.9 61.4 %copy-start.4 = (s32[16384]{0:T(1024)}, s32[16384]{0:T(1024)S(1)}, u32[]{:S(2)}) copy-start(s32[16384]{0:T(1024)S(1)} %fusion.2) | copy-start | bytes 196612
  1.8 60.5 %copy-start.8 = (pred[16384]{0:T(1024)(128)(4,1)}, pred[16384]{0:T(1024)(128)(4,1)S(1)}, u32[]{:S(2)}) copy-start(pred[16384]{0:T(1024)(128)(4,1)S(1)} %compare_and_fusion) | copy-start | bytes 49156
  79.8 11.5 copy-start.15
  79.8 16.9 copy-start.12
  79.8 52.4 %all-to-all-start = ((bf16[96,128,128]{2,0,1:T(8,128)(2,1)}), bf16[96,128,128]{2,0,1:T(8,128)(2,1)S(1)}, u32[]{:S(2)}, u32[]{:S(2)}) async-start(bf16[96,128,128]{2,0,1:T(8,128)(2,1)} %copy.59), calls=%async_computation | async-start | bytes 6291456 | tf_op jit(solution)/shard_map/all_to_all | solution.py:34
  132.2 1.4 copy-start.2
  150.6 799.9 %copy-start.6 = (pred[8192]{0:T(1024)(128)(4,1)S(1)}, pred[8192]{0:T(1024)(128)(4,1)}, u32[]{:S(2)}) copy-start(pred[8192]{0:T(1024)(128)(4,1)} %iota_compare_fusion) | copy-start | bytes 24580
  950.5 128.0 %copy-start = (f32[96,8192]{1,0:T(8,128)}, f32[96,8192]{1,0:T(8,128)S(1)}, u32[]{:S(2)}) copy-start(f32[96,8192]{1,0:T(8,128)S(1)} %get-tuple-element.194) | copy-start | bytes 9437188
  950.5 128.0 %copy-start.13 = (f32[2,96]{1,0:T(2,128)S(1)}, f32[2,96]{1,0:T(2,128)}, u32[]{:S(2)}) copy-start(f32[2,96]{1,0:T(2,128)} %param.20) | copy-start | bytes 2308
  950.6 128.0 %copy-start.10 = (f32[96]{0:T(128)S(1)}, f32[96]{0:T(128)}, u32[]{:S(2)}) copy-start(f32[96]{0:T(128)} %get-tuple-element.257) | copy-start | bytes 1156
  1078.6 4.9 copy-start.5
  1083.5 57.4 %copy-start.9 = (pred[16384]{0:T(1024)(128)(4,1)S(1)}, pred[16384]{0:T(1024)(128)(4,1)}, u32[]{:S(2)}) copy-start(pred[16384]{0:T(1024)(128)(4,1)} %copy-done.8) | copy-start | bytes 49156
  1158.4 7.8 copy-start.1
  1158.4 46.3 %all-to-all-start.1 = ((bf16[96,128,128]{2,0,1:T(8,128)(2,1)}), bf16[96,128,128]{2,0,1:T(8,128)(2,1)}, u32[]{:S(2)}, u32[]{:S(2)}) async-start(bf16[96,128,128]{2,0,1:T(8,128)(2,1)} %copy.64), calls=%async_computation.1 | async-start | bytes 6291456 | tf_op jit(solution)/shard_map/all_to_all | solution.py:34
  1168.1 38.8 %copy-start.3 = (bf16[96,8192]{1,0:T(8,128)(2,1)S(1)}, bf16[96,8192]{1,0:T(8,128)(2,1)}, u32[]{:S(2)}) copy-start(bf16[96,8192]{1,0:T(8,128)(2,1)} %select_convert_fusion.1) | copy-start | bytes 4718596
  1223.9 799.9 %copy-start.7 = (pred[8192]{0:T(1024)(128)(4,1)S(1)}, pred[8192]{0:T(1024)(128)(4,1)}, u32[]{:S(2)}) copy-start(pred[8192]{0:T(1024)(128)(4,1)} %iota_compare_fusion) | copy-start | bytes 24580
  2023.9 127.8 %copy-start.14 = (f32[2,96]{1,0:T(2,128)S(1)}, f32[2,96]{1,0:T(2,128)}, u32[]{:S(2)}) copy-start(f32[2,96]{1,0:T(2,128)} %param.20) | copy-start | bytes 2308
  2023.9 127.8 %copy-start.11 = (f32[96]{0:T(128)S(1)}, f32[96]{0:T(128)}, u32[]{:S(2)}) copy-start(f32[96]{0:T(128)} %get-tuple-element.256) | copy-start | bytes 1156
where the time goes:
time: 2160 us; the launch traced here: 2150 us
  local copies, waits for them, and re-layouts  1690 us (78%)
  blocking collectives  254 us (12%)
  matrix products  76 us (4%)
  waiting for transfers between devices  71.7 us (3%)
  other arithmetic  46.9 us (2%)
    gather x8, local copies, waits for them, and re-layouts, advance(): gathered = jnp.take(table, columns, axis=0, mode='clip')  1500 us
    psum x2, blocking collectives, normalize(): average = lax.psum(jnp.sum(masked, axis=1), ('region', 'sub')) / population  128 us
    psum x2, blocking collectives, normalize(): lax.psum(jnp.sum(offset * offset, axis=1), ('region', 'sub')) / population  125 us
    gather x2, local copies, waits for them, and re-layouts, route(): parcel = jnp.transpose(jnp.take(jnp.transpose(hidden), outgoing, axis=0))  115 us
    dot_general x8, matrix products, advance(): jnp.einsum('kbi,kio->ob', gathered, weight, preferred_element_type=jnp.fl...  76 us
    all_to_all x2, waiting for transfers between devices, route(): lax.all_to_all(parcel, ('region', 'sub'), split_axis=1, concat_axis=1, ti...  71.7 us
  transfers between devices with their start and end apart: 2, of which 2 were waited for; matrix products, arithmetic and copies ran while one was open for 0% of the time, Pallas kernels for 0%

commit v1 on v0

v1 whole, which is shorter than its diff:
```python
import functools

import jax
import jax.numpy as jnp
from jax import lax
from jax.experimental import pallas as pl
from jax.experimental.pallas import tpu as pltpu
from jax.sharding import PartitionSpec as P

AXES = ("region", "sub")
C = 96
K3 = 27
MID = K3 // 2
PAIRS = MID
BLOCK = 128
LANES = 128
V_DEV = 8192
CAP = 128
DEVICES = 128
ARRIVED = DEVICES * CAP
MISSING = V_DEV + ARRIVED
NORM_EPS = 1e-05
VMEM_LIMIT = 60 << 20
TAIL = CAP - C
LOW = 0x7FFF

F32 = jnp.float32
BF16 = jnp.bfloat16
IN_VMEM = pl.BlockSpec(memory_space=pltpu.VMEM)
IN_SMEM = pl.BlockSpec(memory_space=pltpu.SMEM)
IN_ANY = pl.BlockSpec(memory_space=pl.ANY)


def moments(stats, counts):
    means, squares = stats[:, 0, :], stats[:, 1, :]
    population = jnp.sum(counts, axis=0, keepdims=True)
    average = jnp.sum(means * counts, axis=0, keepdims=True) / population
    apart = means - average
    spread = jnp.sum(squares + counts * apart * apart, axis=0, keepdims=True) / population
    return average, spread


def send_rows_packed(picks, table, stage, out):
    lane = lax.broadcasted_iota(jnp.int32, (TAIL, LANES), 1)

    def pack(d, slot):
        last = stage[slot, C:CAP, :]
        for j in range(C // TAIL):
            rows = stage[slot, j * TAIL : (j + 1) * TAIL, :]
            moved = pltpu.roll(last, C - j * TAIL, 1) if j < C // TAIL else last
            out[d, j * TAIL : (j + 1) * TAIL, :] = jnp.where(lane < C, rows, moved).astype(BF16)

    def collect(d, slot):
        for c in range(CAP // 2):
            both = picks[d, c]
            stage[slot, c : c + 1, :] = table[pl.ds(both & LOW, 1), :]
            stage[slot, c + CAP // 2 : c + CAP // 2 + 1, :] = table[pl.ds(both >> 16, 1), :]

    collect(0, 0)

    def advance(d, carry):
        pack(d - 1, (d - 1) % 2)
        collect(d, d % 2)
        return carry

    lax.fori_loop(1, DEVICES, advance, 0)
    pack(DEVICES - 1, (DEVICES - 1) % 2)


def first_send_kernel(picks, own, out, table, stage):
    def fill(b, carry):
        rows = pl.ds(pl.multiple_of(b * BLOCK, BLOCK), BLOCK)
        table[rows, 0:C] = own[rows, :].astype(F32)
        return carry

    table[:, C:LANES] = jnp.zeros((V_DEV, LANES - C), F32)
    lax.fori_loop(0, V_DEV // BLOCK, fill, 0)
    send_rows_packed(picks, table, stage, out)


def next_send_kernel(picks, live, conved, stats, counts, gain, shift, out, own, table, stage):
    average, spread = moments(stats, counts[...])
    factor = gain[...] * lax.rsqrt(spread + NORM_EPS)
    offset = shift[...]
    blocks = live[0] // BLOCK

    def fill(b, carry):
        rows = pl.ds(pl.multiple_of(b * BLOCK, BLOCK), BLOCK)
        normed = (conved[rows, :] - average) * factor + offset
        hidden = jnp.maximum(normed, 0.0).astype(BF16)
        own[rows, :] = hidden
        table[rows, :] = hidden.astype(F32)
        return carry

    def clear(b, carry):
        rows = pl.ds(pl.multiple_of(b * BLOCK, BLOCK), BLOCK)
        own[rows, :] = jnp.zeros((BLOCK, LANES), BF16)
        return carry

    lax.fori_loop(0, blocks, fill, 0)
    lax.fori_loop(blocks, V_DEV // BLOCK, clear, 0)
    send_rows_packed(picks, table, stage, out)


def conv_kernel(live, index_hbm, own, arrived, weight, middle, out, stats, table, stage, index, sem):
    load = pltpu.make_async_copy(index_hbm, index, sem)
    load.start()
    blocks = live[0] // BLOCK
    width = own.shape[1]
    lane = lax.broadcasted_iota(jnp.int32, (TAIL, LANES), 1)

    def fill_own(b, carry):
        rows = pl.ds(pl.multiple_of(b * BLOCK, BLOCK), BLOCK)
        table[rows, 0:width] = own[rows, :].astype(F32)
        if width < LANES:
            table[rows, width:LANES] = jnp.zeros((BLOCK, LANES - width), F32)
        return carry

    def fill_arrived(p, carry):
        base = pl.multiple_of(V_DEV + p * CAP, CAP)
        rows = arrived[p].astype(F32)
        table[pl.ds(base, C), :] = rows
        tail = None
        for j in range(C // TAIL):
            moved = pltpu.roll(rows[j * TAIL : (j + 1) * TAIL], TAIL * (j + 1), 1)
            tail = moved if tail is None else jnp.where(lane < j * TAIL, tail, moved)
        table[pl.ds(base + C, TAIL), :] = tail
        return carry

    lax.fori_loop(0, V_DEV // BLOCK, fill_own, 0)
    lax.fori_loop(0, DEVICES, fill_arrived, 0)
    table[MISSING : MISSING + 8, :] = jnp.zeros((8, LANES), F32)
    load.wait()

    def multiply(slot, p):
        return jnp.dot(stage[slot, p].astype(BF16), weight[p], preferred_element_type=F32)

    def collect(block, slot, p):
        for c in range(BLOCK):
            both = index[block * PAIRS + p, c]
            stage[slot, p, c : c + 1, 0:LANES] = table[pl.ds(both & LOW, 1), :]
            stage[slot, p, c : c + 1, LANES : 2 * LANES] = table[pl.ds(both >> 16, 1), :]

    def center(block):
        rows = pl.ds(pl.multiple_of(block * BLOCK, BLOCK), BLOCK)
        return jnp.dot(table[rows, :].astype(BF16), middle[...], preferred_element_type=F32)

    def finish(block, total, sums):
        out[pl.ds(pl.multiple_of(block * BLOCK, BLOCK), BLOCK), :] = total
        return sums + jnp.sum(total.reshape(BLOCK // 8, 8, LANES), axis=0)

    def first(p, carry):
        collect(0, 0, p)
        return carry

    lax.fori_loop(0, PAIRS, first, 0)

    def advance(block, sums):
        now = block % 2

        def pair(p, total):
            total = total + multiply(1 - now, p)
            collect(block, now, p)
            return total

        total = lax.fori_loop(0, PAIRS, pair, center(block - 1))
        return finish(block - 1, total, sums)

    sums = lax.fori_loop(1, blocks, advance, jnp.zeros((8, LANES), F32))
    last = blocks - 1
    total = center(last)
    for p in range(PAIRS):
        total = total + multiply(last % 2, p)
    sums = finish(last, total, sums)

    count = (blocks * BLOCK).astype(F32)
    average = jnp.sum(sums, axis=0, keepdims=True) / count

    def deviate(block, squares):
        rows = pl.ds(pl.multiple_of(block * BLOCK, BLOCK), BLOCK)
        apart = out[rows, :] - average
        return squares + jnp.sum((apart * apart).reshape(BLOCK // 8, 8, LANES), axis=0)

    squares = lax.fori_loop(0, blocks, deviate, jnp.zeros((8, LANES), F32))
    stats[0:1, :] = average
    stats[1:2, :] = jnp.sum(squares, axis=0, keepdims=True)


def last_kernel(live, conved, stats, counts, gain, shift, out):
    step = pl.program_id(0)
    average, spread = moments(stats, counts[...])
    factor = gain[...] * lax.rsqrt(spread + NORM_EPS)
    size = conved.shape[0]
    row = lax.broadcasted_iota(jnp.int32, (size, LANES), 0) + step * size
    normed = jnp.maximum((conved[...] - average) * factor + shift[...], 0.0)
    normed = jnp.where(row < live[0], normed, 0.0)
    out[...] = jnp.transpose(normed)[0:C, :].astype(BF16)


def params():
    return pltpu.CompilerParams(vmem_limit_bytes=VMEM_LIMIT)


def first_send(picks, own):
    return pl.pallas_call(
        first_send_kernel,
        in_specs=[IN_SMEM, IN_VMEM],
        out_specs=IN_VMEM,
        out_shape=jax.ShapeDtypeStruct((DEVICES, C, LANES), BF16),
        scratch_shapes=[pltpu.VMEM((V_DEV, LANES), F32), pltpu.VMEM((2, CAP, LANES), F32)],
        compiler_params=params(),
        name="first_send",
    )(picks, own)


def next_send(picks, live, conved, stats, counts, gain, shift):
    return pl.pallas_call(
        next_send_kernel,
        in_specs=[IN_SMEM, IN_SMEM] + [IN_VMEM] * 5,
        out_specs=[IN_VMEM, IN_VMEM],
        out_shape=[
            jax.ShapeDtypeStruct((DEVICES, C, LANES), BF16),
            jax.ShapeDtypeStruct((V_DEV, LANES), BF16),
        ],
        scratch_shapes=[pltpu.VMEM((V_DEV, LANES), F32), pltpu.VMEM((2, CAP, LANES), F32)],
        compiler_params=params(),
        name="next_send",
    )(picks, live, conved, stats, counts, gain, shift)


def convolve(live, index, own, arrived, weight, middle):
    return pl.pallas_call(
        conv_kernel,
        in_specs=[IN_SMEM, IN_ANY] + [IN_VMEM] * 4,
        out_specs=[IN_VMEM, IN_VMEM],
        out_shape=[
            jax.ShapeDtypeStruct((V_DEV, LANES), F32),
            jax.ShapeDtypeStruct((2, LANES), F32),
        ],
        scratch_shapes=[
            pltpu.VMEM((MISSING + 8, LANES), F32),
            pltpu.VMEM((2, PAIRS, BLOCK, 2 * LANES), F32),
            pltpu.SMEM((V_DEV // BLOCK * PAIRS, BLOCK), jnp.int32),
            pltpu.SemaphoreType.DMA,
        ],
        compiler_params=params(),
        name="sparse_conv",
    )(live, index, own, arrived, weight, middle)


def last_norm(live, conved, stats, counts, gain, shift):
    size = 1024
    whole = lambda *dims: pl.BlockSpec(dims, lambda i: (0,) * len(dims))
    return pl.pallas_call(
        last_kernel,
        grid=(V_DEV // size,),
        in_specs=[
            IN_SMEM,
            pl.BlockSpec((size, LANES), lambda i: (i, 0)),
            whole(DEVICES, 2, LANES),
            whole(DEVICES, LANES),
            whole(1, LANES),
            whole(1, LANES),
        ],
        out_specs=pl.BlockSpec((C, size), lambda i: (0, i)),
        out_shape=jax.ShapeDtypeStruct((C, V_DEV), BF16),
        compiler_params=params(),
        name="last_norm",
    )(live, conved, stats, counts, gain, shift)


def exchange(parcels):
    return lax.all_to_all(parcels, AXES, split_axis=0, concat_axis=0, tiled=True)


def share(stats):
    return exchange(jnp.broadcast_to(stats[None], (DEVICES, 2, LANES)))


def prepare_weight(weight):
    wide = jnp.pad(weight, ((0, 0), (0, LANES - C), (0, LANES - C)))
    return jnp.concatenate([wide[:MID], wide[MID + 1 :]], axis=1), wide[MID]


def body(
    features, neighbors, send_rows, active_rows, weight_one, weight_two, norm_gain, norm_shift
):
    device = lax.axis_index(AXES)
    live = lax.dynamic_slice_in_dim(active_rows, device, 1)
    counts = jnp.broadcast_to(active_rows.astype(F32)[:, None], (DEVICES, LANES))
    gain = jnp.pad(norm_gain, ((0, 0), (0, LANES - C)))
    shift = jnp.pad(norm_shift, ((0, 0), (0, LANES - C)))
    listed = send_rows.reshape(DEVICES, CAP)
    picks = listed[:, : CAP // 2] | (listed[:, CAP // 2 :] << 16)
    index = neighbors[:MID] | (neighbors[MID + 1 :] << 16)
    index = index.reshape(PAIRS, V_DEV // BLOCK, BLOCK).transpose(1, 0, 2).reshape(-1, BLOCK)

    own = jnp.transpose(features)
    arrived = exchange(first_send(picks, own))
    conved, stats = convolve(live, index, own, arrived, *prepare_weight(weight_one))
    stats = share(stats)
    parcels, own = next_send(picks, live, conved, stats, counts, gain[0:1], shift[0:1])
    arrived = exchange(parcels)
    conved, stats = convolve(live, index, own, arrived, *prepare_weight(weight_two))
    stats = share(stats)
    return last_norm(live, conved, stats, counts, gain[1:2], shift[1:2])


def solution(mesh):
    placed = (
        P(None, AXES),
        P(None, AXES),
        P(AXES, None),
        P(),
        P(),
        P(),
        P(),
        P(),
    )
    return jax.shard_map(
        body, mesh=mesh, in_specs=placed, out_specs=P(None, AXES), check_vma=False
    )
```

time: 2160 us -> 607 us (0.28)
  local copies, waits for them, and re-layouts: 1690 us -> 19.6 us
  Pallas kernels: 0 us -> 415 us
  blocking collectives: 254 us -> 41.6 us
  matrix products: 76 us -> 0 us
  other arithmetic: 46.9 us -> 4.01 us
  starting transfers between devices: 17.2 us -> 46.8 us
    gather x10 -> x0, local copies, waits for them, and re-layouts: 1620 us -> none  [the longest x8 1500 us: advance(): gathered = jnp.take(table, columns, axis=0, mode='clip')]
    pallas_call x0 -> x5, Pallas kernels: none -> 415 us  [the longest x2 365 us: convolve(): pl.pallas_call(conv_kernel, in_specs=[IN_SMEM, IN_ANY] + [IN_VMEM] * 4, o...]
    psum x4 -> x0, blocking collectives: 254 us -> none  [the longest x2 128 us: normalize(): average = lax.psum(jnp.sum(masked, axis=1), ('region', 'sub')) / population]
    dot_general x8 -> x0, matrix products: 76 us -> none  [advance(): jnp.einsum('kbi,kio->ob', gathered, weight, preferred_element_type=jnp.fl...]
    all_to_all x0 -> x1, blocking collectives: none -> 41.6 us  [exchange(): lax.all_to_all(parcels, AXES, split_axis=0, concat_axis=0, tiled=True)]
    all_to_all x2 -> x3, starting transfers between devices: 17.2 us -> 46.8 us  [exchange(): lax.all_to_all(parcels, AXES, split_axis=0, concat_axis=0, tiled=True)]
    select_n x2 -> x0, other arithmetic: 23 us -> none  [route(): parcel = jnp.transpose(jnp.take(jnp.transpose(hidden), outgoing, axis=0))]
    all_to_all x2 -> x3, waiting for transfers between devices: 71.7 us -> 79 us  [exchange(): lax.all_to_all(parcels, AXES, split_axis=0, concat_axis=0, tiled=True)]
  transfers between devices with their start and end apart: 2 -> 3, of which waited for: 2 -> 3; matrix products, arithmetic and copies ran while one was open for 0% -> 2% of each run, Pallas kernels for 0% -> 0%
where the time goes in v1:
time: 607 us
  Pallas kernels  415 us (68%)
  waiting for transfers between devices  79 us (13%)
  starting transfers between devices  46.8 us (8%)
  blocking collectives  41.6 us (7%)
  local copies, waits for them, and re-layouts  19.6 us (3%)
    pallas_call x2, Pallas kernels, convolve(): pl.pallas_call(conv_kernel, in_specs=[IN_SMEM, IN_ANY] + [IN_VMEM] * 4, o...  365 us
    all_to_all x3, waiting for transfers between devices, exchange(): lax.all_to_all(parcels, AXES, split_axis=0, concat_axis=0, tiled=True)  79 us
    all_to_all x3, starting transfers between devices, exchange(): lax.all_to_all(parcels, AXES, split_axis=0, concat_axis=0, tiled=True)  46.8 us
    all_to_all x1, blocking collectives, exchange(): lax.all_to_all(parcels, AXES, split_axis=0, concat_axis=0, tiled=True)  41.6 us
    pallas_call x1, Pallas kernels, next_send(): pl.pallas_call(next_send_kernel, in_specs=[IN_SMEM, IN_SMEM] + [IN_VMEM]...  22.2 us
    pallas_call x1, Pallas kernels, first_send(): pl.pallas_call(first_send_kernel, in_specs=[IN_SMEM, IN_VMEM], out_specs=...  20.1 us
  transfers between devices with their start and end apart: 3, of which 3 were waited for; matrix products, arithmetic and copies ran while one was open for 2% of the time, Pallas kernels for 0%

profile of v1, /device:TPU:1, one launch (start us, length us, event | category | flops | bytes accessed | tf_op | source)
XLA Modules:
  0.0 606.5 jit_solution(2350696199459106474)
XLA Ops:
  0.0 3.9 copy.12
  3.9 0.7 fusion.picks
  4.6 20.1 %first_send.1 = bf16[128,96,128]{2,1,0:T(8,128)(2,1)} custom-call(s32[128,64]{1,0:T(8,128)} %fusion.picks, bf16[8192,96]{1,0:T(8,128)(2,1)} %bitcast.12), custom_call_target="tpu_custom_call" | custom-call | tf_op jit(solution)/shard_map/first_send/pallas_call | solution.py:205
  24.7 11.5 %all-to-all-start = ((bf16[128,96,128]{2,1,0:T(8,128)(2,1)}), bf16[128,96,128]{2,1,0:T(8,128)(2,1)S(1)}, u32[]{:S(2)}, u32[]{:S(2)}) async-start(bf16[128,96,128]{2,1,0:T(8,128)(2,1)} %first_send.1), calls=%async_computation | async-start | bytes 6291456 | tf_op jit(solution)/shard_map/all_to_all | solution.py:273
  36.2 1.4 shift-left_or_fusion
  37.6 0.0 copy-start.6
  37.6 0.1 copy.13
  37.8 1.0 copy.15
  38.8 1.9 reshape.13.index_hbm
  40.7 0.6 dynamic_slice.3.live
  41.3 1.4 fusion.1.middle
  42.6 1.3 pad_slice_fusion.5
  43.9 1.0 pad_maximum_fusion.weight
  44.9 32.3 %all-to-all-done.arrived = bf16[128,96,128]{2,1,0:T(8,128)(2,1)S(1)} async-done(((bf16[128,96,128]{2,1,0:T(8,128)(2,1)}), bf16[128,96,128]{2,1,0:T(8,128)(2,1)S(1)}, u32[]{:S(2)}, u32[]{:S(2)}) %all-to-all-start) | async-done | bytes 3145760 | tf_op jit(solution)/shard_map/all_to_all | solution.py:273
  77.1 1.7 copy-done
  78.8 182.8 %sparse_conv.2 = (f32[8192,128]{1,0:T(8,128)}, f32[2,128]{1,0:T(2,128)}) custom-call(s32[1]{0:T(128)} %dynamic_slice.3.live, s32[832,128]{1,0:T(8,128)} %reshape.13.index_hbm, bf16[8192,96]{1,0:T(8,128)(2,1)} %bitcast.13, bf16[128,96,128]{2,1,0:T(8,128)(2,1)} %copy-done, bf16[13,256,128]{2,1,0:T(8,128)(2,1)} %pad_maximum_fusion.weight, ...), custom_call_target="tpu_custom_call" | custom-call | tf_op jit(solution)/shard_map/sparse_conv/pallas_call | solution.py:232
  261.7 1.4 broadcast_in_dim.6
  263.0 31.4 %all-to-all-start.1 = ((f32[128,2,128]{2,1,0:T(2,128)}), f32[128,2,128]{2,1,0:T(2,128)S(1)}, u32[]{:S(2)}, u32[]{:S(2)}) async-start(f32[128,2,128]{2,1,0:T(2,128)} %broadcast_in_dim.6), calls=%async_computation.1 | async-start | bytes 262144 | tf_op jit(solution)/shard_map/all_to_all | solution.py:273
  294.5 0.6 pad_slice_fusion.6
  295.1 9.4 %all-to-all-done.1.stats = f32[128,2,128]{2,1,0:T(2,128)S(1)} async-done(((f32[128,2,128]{2,1,0:T(2,128)}), f32[128,2,128]{2,1,0:T(2,128)S(1)}, u32[]{:S(2)}, u32[]{:S(2)}) %all-to-all-start.1) | async-done | bytes 131104 | tf_op jit(solution)/shard_map/all_to_all | solution.py:273
  304.5 0.7 broadcast_in_dim.7.counts
  305.2 22.2 %next_send.1 = (bf16[128,96,128]{2,1,0:T(8,128)(2,1)}, bf16[8192,128]{1,0:T(8,128)(2,1)}) custom-call(s32[128,64]{1,0:T(8,128)} %fusion.picks, s32[1]{0:T(128)} %dynamic_slice.3.live, f32[8192,128]{1,0:T(8,128)} %get-tuple-element.11.conved, f32[128,2,128]{2,1,0:T(2,128)} %copy-done.2, f32[128,128]{1,0:T(8,128)} %broadcast_in_dim.7.counts, ...), custom_call_target="tpu_custom_call" | custom-call | tf_op jit(solution)/shard_map/next_send/pallas_call | solution.py:217
  327.4 3.9 all-to-all-start.2
  331.3 1.4 fusion.2.middle
  332.7 1.3 pad_slice_fusion.2
  334.0 1.0 pad_maximum_fusion.1.weight
  335.0 37.3 %all-to-all-done.2.arrived = bf16[128,96,128]{2,1,0:T(8,128)(2,1)S(1)} async-done(((bf16[128,96,128]{2,1,0:T(8,128)(2,1)}), bf16[128,96,128]{2,1,0:T(8,128)(2,1)S(1)}, u32[]{:S(2)}, u32[]{:S(2)}) %all-to-all-start.2) | async-done | bytes 3145760 | tf_op jit(solution)/shard_map/all_to_all | solution.py:273
  372.3 1.7 copy-done.1
  373.9 182.5 %sparse_conv.3 = (f32[8192,128]{1,0:T(8,128)}, f32[2,128]{1,0:T(2,128)}) custom-call(s32[1]{0:T(128)} %dynamic_slice.3.live, s32[832,128]{1,0:T(8,128)} %reshape.13.index_hbm, bf16[8192,128]{1,0:T(8,128)(2,1)} %get-tuple-element.13.own, bf16[128,96,128]{2,1,0:T(8,128)(2,1)} %copy-done.1, bf16[13,256,128]{2,1,0:T(8,128)(2,1)} %pad_maximum_fusion.1.weight, ...), custom_call_target="tpu_custom_call" | custom-call | tf_op jit(solution)/shard_map/sparse_conv/pallas_call | solution.py:232
  556.5 0.7 broadcast_in_dim.8
  557.2 41.6 %all_to_all.20.stats = f32[128,2,128]{2,1,0:T(2,128)} all-to-all(f32[128,2,128]{2,1,0:T(2,128)S(1)} %broadcast_in_dim.8), channel_id=1, replica_groups=mesh['region'=8,'sub'=16] {'region','sub'}, dimensions={0} | all-to-all | bytes 262144 | tf_op jit(solution)/shard_map/all_to_all | solution.py:273
  598.8 7.7 %last_norm.1 = bf16[96,8192]{1,0:T(8,128)(2,1)} custom-call(s32[1]{0:T(128)} %dynamic_slice.3.live, f32[8192,128]{1,0:T(8,128)} %get-tuple-element.15.conved, f32[128,2,128]{2,1,0:T(2,128)} %all_to_all.20.stats, f32[128,128]{1,0:T(8,128)} %broadcast_in_dim.7.counts, f32[1,128]{1,0:T(1,128)} %get-tuple-element.26.gain, f32[1,128]{1,0:T(1,128)} %get-tuple-element.21.shift), custom_call_target="tpu_custom_call" | custom-call | tf_op jit(solution)/shard_map/last_norm/pallas_call | solution.py:254
  (13 shorter events, 0.1 us)
Async XLA Ops:
  0.0 3.9 copy-start.3
  24.7 52.4 %all-to-all-start = ((bf16[128,96,128]{2,1,0:T(8,128)(2,1)}), bf16[128,96,128]{2,1,0:T(8,128)(2,1)S(1)}, u32[]{:S(2)}, u32[]{:S(2)}) async-start(bf16[128,96,128]{2,1,0:T(8,128)(2,1)} %first_send.1), calls=%async_computation | async-start | bytes 6291456 | tf_op jit(solution)/shard_map/all_to_all | solution.py:273
  37.6 3.1 copy-start.6
  44.9 249.6 %copy-start.4 = (f32[2,96]{1,0:T(2,128)S(1)}, f32[2,96]{1,0:T(2,128)}, u32[]{:S(2)}) copy-start(f32[2,96]{1,0:T(2,128)} %param.15) | copy-start | bytes 2308
  44.9 249.6 %copy-start.5 = (f32[2,96]{1,0:T(2,128)S(1)}, f32[2,96]{1,0:T(2,128)}, u32[]{:S(2)}) copy-start(f32[2,96]{1,0:T(2,128)} %param.14) | copy-start | bytes 2308
  77.1 1.7 copy-start
  263.0 41.5 %all-to-all-start.1 = ((f32[128,2,128]{2,1,0:T(2,128)}), f32[128,2,128]{2,1,0:T(2,128)S(1)}, u32[]{:S(2)}, u32[]{:S(2)}) async-start(f32[128,2,128]{2,1,0:T(2,128)} %broadcast_in_dim.6), calls=%async_computation.1 | async-start | bytes 262144 | tf_op jit(solution)/shard_map/all_to_all | solution.py:273
  304.5 0.7 copy-start.2
  327.4 44.9 %all-to-all-start.2 = ((bf16[128,96,128]{2,1,0:T(8,128)(2,1)}), bf16[128,96,128]{2,1,0:T(8,128)(2,1)S(1)}, u32[]{:S(2)}, u32[]{:S(2)}) async-start(bf16[128,96,128]{2,1,0:T(8,128)(2,1)} %get-tuple-element.14), calls=%async_computation.2 | async-start | bytes 6291456 | tf_op jit(solution)/shard_map/all_to_all | solution.py:273
  372.3 1.7 copy-start.1

commit v2 on v1

--- a/solution.py
+++ b/solution.py
@@ -16,13 +16,14 @@
 LANES = 128
 V_DEV = 8192
 CAP = 128
+GROUP = 8
+SLOTS = 4
 DEVICES = 128
 ARRIVED = DEVICES * CAP
 MISSING = V_DEV + ARRIVED
 NORM_EPS = 1e-05
 VMEM_LIMIT = 60 << 20
 TAIL = CAP - C
-LOW = 0x7FFF
 
 F32 = jnp.float32
 BF16 = jnp.bfloat16
@@ -40,45 +41,64 @@
     return average, spread
 
 
-def send_rows_packed(picks, table, stage, out):
+def send_rows_packed(picks, table, stage, out, index, sems):
     lane = lax.broadcasted_iota(jnp.int32, (TAIL, LANES), 1)
-
-    def pack(d, slot):
-        last = stage[slot, C:CAP, :]
-        for j in range(C // TAIL):
-            rows = stage[slot, j * TAIL : (j + 1) * TAIL, :]
-            moved = pltpu.roll(last, C - j * TAIL, 1) if j < C // TAIL else last
-            out[d, j * TAIL : (j + 1) * TAIL, :] = jnp.where(lane < C, rows, moved).astype(BF16)
-
-    def collect(d, slot):
-        for c in range(CAP // 2):
-            both = picks[d, c]
-            stage[slot, c : c + 1, :] = table[pl.ds(both & LOW, 1), :]
-            stage[slot, c + CAP // 2 : c + CAP // 2 + 1, :] = table[pl.ds(both >> 16, 1), :]
-
-    collect(0, 0)
-
-    def advance(d, carry):
-        pack(d - 1, (d - 1) % 2)
-        collect(d, d % 2)
-        return carry
-
-    lax.fori_loop(1, DEVICES, advance, 0)
-    pack(DEVICES - 1, (DEVICES - 1) % 2)
-
-
-def first_send_kernel(picks, own, out, table, stage):
+    groups = DEVICES // GROUP
+
+    def fetch(g, slot):
+        return pltpu.make_async_copy(picks.at[g], index.at[slot], sems.at[slot])
+
+    def pack(d, j):
+        last = stage[j, C:CAP, :]
+        for t in range(C // TAIL):
+            rows = stage[j, t * TAIL : (t + 1) * TAIL, :]
+            moved = pltpu.roll(last, C - t * TAIL, 1)
+            out[d, t * TAIL : (t + 1) * TAIL, :] = jnp.where(lane < C, rows, moved).astype(BF16)
+
+    def group(g, slot):
+        for j in range(GROUP):
+            pack(jnp.maximum(g - 1, 0) * GROUP + j, j)
+            for c in range(CAP):
+                stage[j, c : c + 1, :] = table[pl.ds(index[slot, j, c], 1), :]
+
+    def advance(r, carry):
+        for slot in range(SLOTS):
+            g = r * SLOTS + slot
+            fetch(g, slot).wait()
+            group(g, slot)
+
+            @pl.when(g + SLOTS < groups)
+            def _():
+                fetch(g + SLOTS, slot).start()
+
+        return carry
+
+    lax.fori_loop(0, groups // SLOTS, advance, 0)
+    for j in range(GROUP):
+        pack(DEVICES - GROUP + j, j)
+
+
+def start_picks(picks, index, sems):
+    for slot in range(SLOTS):
+        pltpu.make_async_copy(picks.at[slot], index.at[slot], sems.at[slot]).start()
+
+
+def first_send_kernel(picks, own, out, table, stage, index, sems):
+    start_picks(picks, index, sems)
+
     def fill(b, carry):
         rows = pl.ds(pl.multiple_of(b * BLOCK, BLOCK), BLOCK)
-        table[rows, 0:C] = own[rows, :].astype(F32)
-        return carry
-
-    table[:, C:LANES] = jnp.zeros((V_DEV, LANES - C), F32)
+        table[rows, :] = own[rows, :].astype(F32)
+        return carry
+
     lax.fori_loop(0, V_DEV // BLOCK, fill, 0)
-    send_rows_packed(picks, table, stage, out)
-
-
-def next_send_kernel(picks, live, conved, stats, counts, gain, shift, out, own, table, stage):
+    send_rows_packed(picks, table, stage, out, index, sems)
+
+
+def next_send_kernel(
+    picks, live, conved, stats, counts, gain, shift, out, own, table, stage, index, sems
+):
+    start_picks(picks, index, sems)
     average, spread = moments(stats, counts[...])
     factor = gain[...] * lax.rsqrt(spread + NORM_EPS)
     offset = shift[...]
@@ -99,21 +119,21 @@
 
     lax.fori_loop(0, blocks, fill, 0)
     lax.fori_loop(blocks, V_DEV // BLOCK, clear, 0)
-    send_rows_packed(picks, table, stage, out)
-
-
-def conv_kernel(live, index_hbm, own, arrived, weight, middle, out, stats, table, stage, index, sem):
-    load = pltpu.make_async_copy(index_hbm, index, sem)
-    load.start()
+    send_rows_packed(picks, table, stage, out, index, sems)
+
+
+def conv_kernel(live, maps, own, arrived, weight, middle, out, stats, table, stage, sums, index, sems):
+    def fetch(block, slot):
+        columns = pl.ds(pl.multiple_of(block * BLOCK, BLOCK), BLOCK)
+        return pltpu.make_async_copy(maps.at[:, columns], index.at[slot], sems.at[slot])
+
+    fetch(0, 0).start()
     blocks = live[0] // BLOCK
-    width = own.shape[1]
     lane = lax.broadcasted_iota(jnp.int32, (TAIL, LANES), 1)
 
     def fill_own(b, carry):
         rows = pl.ds(pl.multiple_of(b * BLOCK, BLOCK), BLOCK)
-        table[rows, 0:width] = own[rows, :].astype(F32)
-        if width < LANES:
-            table[rows, width:LANES] = jnp.zeros((BLOCK, LANES - width), F32)
+        table[rows, :] = own[rows, :].astype(F32)
         return carry
 
     def fill_arrived(p, carry):
@@ -130,51 +150,54 @@
     lax.fori_loop(0, V_DEV // BLOCK, fill_own, 0)
     lax.fori_loop(0, DEVICES, fill_arrived, 0)
     table[MISSING : MISSING + 8, :] = jnp.zeros((8, LANES), F32)
-    load.wait()
 
     def multiply(slot, p):
         return jnp.dot(stage[slot, p].astype(BF16), weight[p], preferred_element_type=F32)
 
-    def collect(block, slot, p):
+    def collect(slot, p):
         for c in range(BLOCK):
-            both = index[block * PAIRS + p, c]
-            stage[slot, p, c : c + 1, 0:LANES] = table[pl.ds(both & LOW, 1), :]
-            stage[slot, p, c : c + 1, LANES : 2 * LANES] = table[pl.ds(both >> 16, 1), :]
+            low, high = index[slot, p, c], index[slot, MID + 1 + p, c]
+            stage[slot, p, c : c + 1, 0:LANES] = table[pl.ds(low, 1), :]
+            stage[slot, p, c : c + 1, LANES : 2 * LANES] = table[pl.ds(high, 1), :]
 
     def center(block):
         rows = pl.ds(pl.multiple_of(block * BLOCK, BLOCK), BLOCK)
         return jnp.dot(table[rows, :].astype(BF16), middle[...], preferred_element_type=F32)
 
-    def finish(block, total, sums):
+    def finish(block, total):
         out[pl.ds(pl.multiple_of(block * BLOCK, BLOCK), BLOCK), :] = total
-        return sums + jnp.sum(total.reshape(BLOCK // 8, 8, LANES), axis=0)
-
-    def first(p, carry):
-        collect(0, 0, p)
-        return carry
-
-    lax.fori_loop(0, PAIRS, first, 0)
-
-    def advance(block, sums):
-        now = block % 2
-
-        def pair(p, total):
-            total = total + multiply(1 - now, p)
-            collect(block, now, p)
-            return total
-
-        total = lax.fori_loop(0, PAIRS, pair, center(block - 1))
-        return finish(block - 1, total, sums)
-
-    sums = lax.fori_loop(1, blocks, advance, jnp.zeros((8, LANES), F32))
+        return jnp.sum(total.reshape(BLOCK // 8, 8, LANES), axis=0)
+
+    def step(block, slot):
+        fetch(block, slot).wait()
+
+        @pl.when(block + 1 < blocks)
+        def _():
+            fetch(block + 1, 1 - slot).start()
+
+        before = jnp.maximum(block - 1, 0)
+        total = center(before)
+        for p in range(PAIRS):
+            total = total + multiply(1 - slot, p)
+            collect(slot, p)
+        part = finish(before, total)
+        sums[...] = jnp.where(block > 0, sums[...] + part, 0.0)
+
+    def advance(block, carry):
+        for slot in range(2):
+            pl.when(block % 2 == slot)(functools.partial(step, block, slot))
+        return carry
+
+    sums[...] = jnp.zeros((8, LANES), F32)
+    lax.fori_loop(0, blocks, advance, 0)
     last = blocks - 1
     total = center(last)
     for p in range(PAIRS):
         total = total + multiply(last % 2, p)
-    sums = finish(last, total, sums)
+    sums[...] += finish(last, total)
 
     count = (blocks * BLOCK).astype(F32)
-    average = jnp.sum(sums, axis=0, keepdims=True) / count
+    average = jnp.sum(sums[...], axis=0, keepdims=True) / count
 
     def deviate(block, squares):
         rows = pl.ds(pl.multiple_of(block * BLOCK, BLOCK), BLOCK)
@@ -201,13 +224,22 @@
     return pltpu.CompilerParams(vmem_limit_bytes=VMEM_LIMIT)
 
 
+def send_scratch():
+    return [
+        pltpu.VMEM((V_DEV, LANES), F32),
+        pltpu.VMEM((GROUP, CAP, LANES), F32),
+        pltpu.SMEM((SLOTS, GROUP, CAP), jnp.int32),
+        pltpu.SemaphoreType.DMA((SLOTS,)),
+    ]
+
+
 def first_send(picks, own):
     return pl.pallas_call(
         first_send_kernel,
-        in_specs=[IN_SMEM, IN_VMEM],
+        in_specs=[IN_ANY, IN_VMEM],
         out_specs=IN_VMEM,
         out_shape=jax.ShapeDtypeStruct((DEVICES, C, LANES), BF16),
-        scratch_shapes=[pltpu.VMEM((V_DEV, LANES), F32), pltpu.VMEM((2, CAP, LANES), F32)],
+        scratch_shapes=send_scratch(),
         compiler_params=params(),
         name="first_send",
     )(picks, own)
@@ -216,19 +248,20 @@
 def next_send(picks, live, conved, stats, counts, gain, shift):
     return pl.pallas_call(
         next_send_kernel,
-        in_specs=[IN_SMEM, IN_SMEM] + [IN_VMEM] * 5,
+        in_specs=[IN_ANY, IN_SMEM] + [IN_VMEM] * 5,
         out_specs=[IN_VMEM, IN_VMEM],
         out_shape=[
             jax.ShapeDtypeStruct((DEVICES, C, LANES), BF16),
             jax.ShapeDtypeStruct((V_DEV, LANES), BF16),
         ],
-        scratch_shapes=[pltpu.VMEM((V_DEV, LANES), F32), pltpu.VMEM((2, CAP, LANES), F32)],
+        scratch_shapes=send_scratch(),
         compiler_params=params(),
         name="next_send",
     )(picks, live, conved, stats, counts, gain, shift)
 
 
-def convolve(live, index, own, arrived, weight, middle):
+@jax.jit
+def convolve(live, maps, own, arrived, weight, middle):
     return pl.pallas_call(
         conv_kernel,
         in_specs=[IN_SMEM, IN_ANY] + [IN_VMEM] * 4,
@@ -240,12 +273,13 @@
         scratch_shapes=[
             pltpu.VMEM((MISSING + 8, LANES), F32),
             pltpu.VMEM((2, PAIRS, BLOCK, 2 * LANES), F32),
-            pltpu.SMEM((V_DEV // BLOCK * PAIRS, BLOCK), jnp.int32),
-            pltpu.SemaphoreType.DMA,
+            pltpu.VMEM((8, LANES), F32),
+            pltpu.SMEM((2, K3, BLOCK), jnp.int32),
+            pltpu.SemaphoreType.DMA((2,)),
         ],
         compiler_params=params(),
         name="sparse_conv",
-    )(live, index, own, arrived, weight, middle)
+    )(live, maps, own, arrived, weight, middle)
 
 
 def last_norm(live, conved, stats, counts, gain, shift):
@@ -290,18 +324,15 @@
     counts = jnp.broadcast_to(active_rows.astype(F32)[:, None], (DEVICES, LANES))
     gain = jnp.pad(norm_gain, ((0, 0), (0, LANES - C)))
     shift = jnp.pad(norm_shift, ((0, 0), (0, LANES - C)))
-    listed = send_rows.reshape(DEVICES, CAP)
-    picks = listed[:, : CAP // 2] | (listed[:, CAP // 2 :] << 16)
-    index = neighbors[:MID] | (neighbors[MID + 1 :] << 16)
-    index = index.reshape(PAIRS, V_DEV // BLOCK, BLOCK).transpose(1, 0, 2).reshape(-1, BLOCK)
-
-    own = jnp.transpose(features)
+    picks = send_rows.reshape(DEVICES // GROUP, GROUP, CAP)
+
+    own = jnp.pad(jnp.transpose(features), ((0, 0), (0, LANES - C)))
     arrived = exchange(first_send(picks, own))
-    conved, stats = convolve(live, index, own, arrived, *prepare_weight(weight_one))
+    conved, stats = convolve(live, neighbors, own, arrived, *prepare_weight(weight_one))
     stats = share(stats)
     parcels, own = next_send(picks, live, conved, stats, counts, gain[0:1], shift[0:1])
     arrived = exchange(parcels)
-    conved, stats = convolve(live, index, own, arrived, *prepare_weight(weight_two))
+    conved, stats = convolve(live, neighbors, own, arrived, *prepare_weight(weight_two))
     stats = share(stats)
     return last_norm(live, conved, stats, counts, gain[1:2], shift[1:2])
 

time: 607 us -> 479 us (0.79)
  Pallas kernels: 415 us -> 184 us
  starting transfers between devices: 46.8 us -> 98.9 us
  blocking collectives: 41.6 us -> 93.1 us
    pallas_call x2, Pallas kernels: 365 us -> 147 us  [convolve(): pl.pallas_call(conv_kernel, in_specs=[IN_SMEM, IN_ANY] + [IN_VMEM] * 4, o...]
    all_to_all x3, starting transfers between devices: 46.8 us -> 98.9 us  [exchange(): lax.all_to_all(parcels, AXES, split_axis=0, concat_axis=0, tiled=True)]
    all_to_all x1, blocking collectives: 41.6 us -> 93.1 us  [exchange(): lax.all_to_all(parcels, AXES, split_axis=0, concat_axis=0, tiled=True)]
    pallas_call x2, Pallas kernels: 42.3 us -> 28.7 us  [the longest x1 15.4 us: next_send(): pl.pallas_call(next_send_kernel, in_specs=[IN_ANY, IN_SMEM] + [IN_VMEM] *...]
where the time goes in v2:
time: 479 us
  Pallas kernels  184 us (38%)
  starting transfers between devices  98.9 us (21%)
  blocking collectives  93.1 us (19%)
  waiting for transfers between devices  83.4 us (17%)
  local copies, waits for them, and re-layouts  17.5 us (4%)
    pallas_call x2, Pallas kernels, convolve(): pl.pallas_call(conv_kernel, in_specs=[IN_SMEM, IN_ANY] + [IN_VMEM] * 4, o...  147 us
    all_to_all x3, starting transfers between devices, exchange(): lax.all_to_all(parcels, AXES, split_axis=0, concat_axis=0, tiled=True)  98.9 us
    all_to_all x1, blocking collectives, exchange(): lax.all_to_all(parcels, AXES, split_axis=0, concat_axis=0, tiled=True)  93.1 us
    all_to_all x3, waiting for transfers between devices, exchange(): lax.all_to_all(parcels, AXES, split_axis=0, concat_axis=0, tiled=True)  83.4 us
    pallas_call x1, Pallas kernels, next_send(): pl.pallas_call(next_send_kernel, in_specs=[IN_ANY, IN_SMEM] + [IN_VMEM] *...  15.4 us
    pallas_call x1, Pallas kernels, first_send(): pl.pallas_call(first_send_kernel, in_specs=[IN_ANY, IN_VMEM], out_specs=I...  13.3 us
  transfers between devices with their start and end apart: 3, of which 3 were waited for; matrix products, arithmetic and copies ran while one was open for 2% of the time, Pallas kernels for 0%

profile of v2, /device:TPU:1, one launch (start us, length us, event | category | flops | bytes accessed | tf_op | source)
XLA Modules:
  0.0 478.7 jit_solution(1490765807176745144)
XLA Ops:
  0.0 3.1 copy.9
  3.1 1.8 pad.18.own
  4.9 13.3 %first_send.1 = bf16[128,96,128]{2,1,0:T(8,128)(2,1)} custom-call(s32[16,8,128]{2,1,0:T(8,128)} %bitcast.7, bf16[8192,128]{1,0:T(8,128)(2,1)} %pad.18.own), custom_call_target="tpu_custom_call" | custom-call | tf_op jit(solution)/shard_map/first_send/pallas_call | solution.py:237
  18.2 0.0 copy-start.5
  18.2 11.5 %all-to-all-start = ((bf16[128,96,128]{2,1,0:T(8,128)(2,1)}), bf16[128,96,128]{2,1,0:T(8,128)(2,1)S(1)}, u32[]{:S(2)}, u32[]{:S(2)}) async-start(bf16[128,96,128]{2,1,0:T(8,128)(2,1)} %first_send.1), calls=%async_computation | async-start | bytes 6291456 | tf_op jit(solution)/shard_map/all_to_all | solution.py:307
  29.7 0.0 copy-done.5
  29.7 0.6 dynamic_slice.3.live
  30.3 1.4 fusion.middle
  31.7 1.3 pad_slice_fusion.5
  33.0 1.0 pad_maximum_fusion.weight
  33.9 36.7 %all-to-all-done.arrived = bf16[128,96,128]{2,1,0:T(8,128)(2,1)S(1)} async-done(((bf16[128,96,128]{2,1,0:T(8,128)(2,1)}), bf16[128,96,128]{2,1,0:T(8,128)(2,1)S(1)}, u32[]{:S(2)}, u32[]{:S(2)}) %all-to-all-start) | async-done | bytes 3145760 | tf_op jit(solution)/shard_map/all_to_all | solution.py:307
  70.6 1.7 copy-done
  72.3 73.7 %sparse_conv.2 = (f32[8192,128]{1,0:T(8,128)}, f32[2,128]{1,0:T(2,128)}) custom-call(s32[1]{0:T(128)} %dynamic_slice.3.live, s32[27,8192]{1,0:T(8,128)} %maps.3, bf16[8192,128]{1,0:T(8,128)(2,1)} %pad.18.own, bf16[128,96,128]{2,1,0:T(8,128)(2,1)} %copy-done, bf16[13,256,128]{2,1,0:T(8,128)(2,1)} %pad_maximum_fusion.weight, bf16[128,128]{1,0:T(8,128)(2,1)} %fusion.middle), custom_call_target="tpu_custom_call" | custom-call | tf_op jit(solution)/shard_map/jit(convolve)/sparse_conv/pallas_call | solution.py:265
  146.0 1.4 broadcast_in_dim.6
  147.4 82.9 %all-to-all-start.1 = ((f32[128,2,128]{2,1,0:T(2,128)}), f32[128,2,128]{2,1,0:T(2,128)S(1)}, u32[]{:S(2)}, u32[]{:S(2)}) async-start(f32[128,2,128]{2,1,0:T(2,128)} %broadcast_in_dim.6), calls=%async_computation.1 | async-start | bytes 262144 | tf_op jit(solution)/shard_map/all_to_all | solution.py:307
  230.3 0.0 copy-done.3
  230.3 0.0 copy-done.4
  230.3 0.6 pad_slice_fusion.6
  230.9 9.4 %all-to-all-done.1.stats = f32[128,2,128]{2,1,0:T(2,128)S(1)} async-done(((f32[128,2,128]{2,1,0:T(2,128)}), f32[128,2,128]{2,1,0:T(2,128)S(1)}, u32[]{:S(2)}, u32[]{:S(2)}) %all-to-all-start.1) | async-done | bytes 131104 | tf_op jit(solution)/shard_map/all_to_all | solution.py:307
  240.3 0.7 broadcast_in_dim.7.counts
  241.0 0.0 copy-done.2
  241.0 15.4 %next_send.1 = (bf16[128,96,128]{2,1,0:T(8,128)(2,1)}, bf16[8192,128]{1,0:T(8,128)(2,1)}) custom-call(s32[16,8,128]{2,1,0:T(8,128)} %bitcast.8, s32[1]{0:T(128)} %dynamic_slice.3.live, f32[8192,128]{1,0:T(8,128)} %get-tuple-element.11.conved, f32[128,2,128]{2,1,0:T(2,128)} %copy-done.2, f32[128,128]{1,0:T(8,128)} %broadcast_in_dim.7.counts, ...), custom_call_target="tpu_custom_call" | custom-call | tf_op jit(solution)/shard_map/next_send/pallas_call | solution.py:249
  256.5 4.5 all-to-all-start.2
  261.0 1.3 fusion.1.middle
  262.3 1.3 pad_slice_fusion.2
  263.6 1.0 pad_maximum_fusion.1.weight
  264.5 37.3 %all-to-all-done.2.arrived = bf16[128,96,128]{2,1,0:T(8,128)(2,1)S(1)} async-done(((bf16[128,96,128]{2,1,0:T(8,128)(2,1)}), bf16[128,96,128]{2,1,0:T(8,128)(2,1)S(1)}, u32[]{:S(2)}, u32[]{:S(2)}) %all-to-all-start.2) | async-done | bytes 3145760 | tf_op jit(solution)/shard_map/all_to_all | solution.py:307
  301.9 1.7 copy-done.1
  303.6 73.7 %sparse_conv.3 = (f32[8192,128]{1,0:T(8,128)}, f32[2,128]{1,0:T(2,128)}) custom-call(s32[1]{0:T(128)} %dynamic_slice.3.live, s32[27,8192]{1,0:T(8,128)} %maps.3, bf16[8192,128]{1,0:T(8,128)(2,1)} %get-tuple-element.13.own, bf16[128,96,128]{2,1,0:T(8,128)(2,1)} %copy-done.1, bf16[13,256,128]{2,1,0:T(8,128)(2,1)} %pad_maximum_fusion.1.weight, ...), custom_call_target="tpu_custom_call" | custom-call | tf_op jit(solution)/shard_map/jit(convolve)/sparse_conv/pallas_call | solution.py:265
  377.2 0.7 broadcast_in_dim.8
  377.9 93.1 %all_to_all.20.stats = f32[128,2,128]{2,1,0:T(2,128)} all-to-all(f32[128,2,128]{2,1,0:T(2,128)S(1)} %broadcast_in_dim.8), channel_id=1, replica_groups=mesh['region'=8,'sub'=16] {'region','sub'}, dimensions={0} | all-to-all | bytes 262144 | tf_op jit(solution)/shard_map/all_to_all | solution.py:307
  471.0 7.7 %last_norm.1 = bf16[96,8192]{1,0:T(8,128)(2,1)} custom-call(s32[1]{0:T(128)} %dynamic_slice.3.live, f32[8192,128]{1,0:T(8,128)} %get-tuple-element.15.conved, f32[128,2,128]{2,1,0:T(2,128)} %all_to_all.20.stats, f32[128,128]{1,0:T(8,128)} %broadcast_in_dim.7.counts, f32[1,128]{1,0:T(1,128)} %get-tuple-element.26.gain, f32[1,128]{1,0:T(1,128)} %get-tuple-element.21.shift), custom_call_target="tpu_custom_call" | custom-call | tf_op jit(solution)/shard_map/last_norm/pallas_call | solution.py:288
  (6 shorter events, 0.0 us)
Async XLA Ops:
  18.2 11.5 %copy-start.5 = (s32[128]{0:T(128)S(1)}, s32[128]{0:T(128)}, u32[]{:S(2)}) copy-start(s32[128]{0:T(128)} %param.11) | copy-start | bytes 1540
  18.2 52.4 %all-to-all-start = ((bf16[128,96,128]{2,1,0:T(8,128)(2,1)}), bf16[128,96,128]{2,1,0:T(8,128)(2,1)S(1)}, u32[]{:S(2)}, u32[]{:S(2)}) async-start(bf16[128,96,128]{2,1,0:T(8,128)(2,1)} %first_send.1), calls=%async_computation | async-start | bytes 6291456 | tf_op jit(solution)/shard_map/all_to_all | solution.py:307
  33.9 196.3 %copy-start.3 = (f32[2,96]{1,0:T(2,128)S(1)}, f32[2,96]{1,0:T(2,128)}, u32[]{:S(2)}) copy-start(f32[2,96]{1,0:T(2,128)} %param.15) | copy-start | bytes 2308
  33.9 196.3 %copy-start.4 = (f32[2,96]{1,0:T(2,128)S(1)}, f32[2,96]{1,0:T(2,128)}, u32[]{:S(2)}) copy-start(f32[2,96]{1,0:T(2,128)} %param.14) | copy-start | bytes 2308
  70.6 1.7 copy-start
  147.4 92.9 %all-to-all-start.1 = ((f32[128,2,128]{2,1,0:T(2,128)}), f32[128,2,128]{2,1,0:T(2,128)S(1)}, u32[]{:S(2)}, u32[]{:S(2)}) async-start(f32[128,2,128]{2,1,0:T(2,128)} %broadcast_in_dim.6), calls=%async_computation.1 | async-start | bytes 262144 | tf_op jit(solution)/shard_map/all_to_all | solution.py:307
  240.3 0.7 copy-start.2
  256.5 45.4 %all-to-all-start.2 = ((bf16[128,96,128]{2,1,0:T(8,128)(2,1)}), bf16[128,96,128]{2,1,0:T(8,128)(2,1)S(1)}, u32[]{:S(2)}, u32[]{:S(2)}) async-start(bf16[128,96,128]{2,1,0:T(8,128)(2,1)} %get-tuple-element.14), calls=%async_computation.2 | async-start | bytes 6291456 | tf_op jit(solution)/shard_map/all_to_all | solution.py:307
  301.9 1.7 copy-start.1

commit v3 on v2

--- a/solution.py
+++ b/solution.py
@@ -32,8 +32,13 @@
 IN_ANY = pl.BlockSpec(memory_space=pl.ANY)
 
 
-def moments(stats, counts):
+def widen(rows):
+    return jnp.concatenate([rows, jnp.zeros((rows.shape[0], LANES - C), rows.dtype)], axis=1)
+
+
+def moments(stats):
     means, squares = stats[:, 0, :], stats[:, 1, :]
+    counts = squares[:, LANES - 1 : LANES]
     population = jnp.sum(counts, axis=0, keepdims=True)
     average = jnp.sum(means * counts, axis=0, keepdims=True) / population
     apart = means - average
@@ -88,7 +93,7 @@
 
     def fill(b, carry):
         rows = pl.ds(pl.multiple_of(b * BLOCK, BLOCK), BLOCK)
-        table[rows, :] = own[rows, :].astype(F32)
+        table[rows, :] = widen(own[rows, :].astype(F32))
         return carry
 
     lax.fori_loop(0, V_DEV // BLOCK, fill, 0)
@@ -96,10 +101,10 @@
 
 
 def next_send_kernel(
-    picks, live, conved, stats, counts, gain, shift, out, own, table, stage, index, sems
+    picks, live, conved, stats, gain, shift, out, own, table, stage, index, sems
 ):
     start_picks(picks, index, sems)
-    average, spread = moments(stats, counts[...])
+    average, spread = moments(stats)
     factor = gain[...] * lax.rsqrt(spread + NORM_EPS)
     offset = shift[...]
     blocks = live[0] // BLOCK
@@ -108,13 +113,13 @@
         rows = pl.ds(pl.multiple_of(b * BLOCK, BLOCK), BLOCK)
         normed = (conved[rows, :] - average) * factor + offset
         hidden = jnp.maximum(normed, 0.0).astype(BF16)
-        own[rows, :] = hidden
+        own[rows, :] = hidden[:, 0:C]
         table[rows, :] = hidden.astype(F32)
         return carry
 
     def clear(b, carry):
         rows = pl.ds(pl.multiple_of(b * BLOCK, BLOCK), BLOCK)
-        own[rows, :] = jnp.zeros((BLOCK, LANES), BF16)
+        own[rows, :] = jnp.zeros((BLOCK, C), BF16)
         return carry
 
     lax.fori_loop(0, blocks, fill, 0)
@@ -133,7 +138,7 @@
 
     def fill_own(b, carry):
         rows = pl.ds(pl.multiple_of(b * BLOCK, BLOCK), BLOCK)
-        table[rows, :] = own[rows, :].astype(F32)
+        table[rows, :] = widen(own[rows, :].astype(F32))
         return carry
 
     def fill_arrived(p, carry):
@@ -147,8 +152,8 @@
         table[pl.ds(base + C, TAIL), :] = tail
         return carry
 
-    lax.fori_loop(0, V_DEV // BLOCK, fill_own, 0)
-    lax.fori_loop(0, DEVICES, fill_arrived, 0)
+    lax.fori_loop(0, V_DEV // BLOCK, fill_own, 0, unroll=2)
+    lax.fori_loop(0, DEVICES, fill_arrived, 0, unroll=8)
     table[MISSING : MISSING + 8, :] = jnp.zeros((8, LANES), F32)
 
     def multiply(slot, p):
@@ -205,13 +210,15 @@
         return squares + jnp.sum((apart * apart).reshape(BLOCK // 8, 8, LANES), axis=0)
 
     squares = lax.fori_loop(0, blocks, deviate, jnp.zeros((8, LANES), F32))
-    stats[0:1, :] = average
-    stats[1:2, :] = jnp.sum(squares, axis=0, keepdims=True)
-
-
-def last_kernel(live, conved, stats, counts, gain, shift, out):
+    spare = lax.broadcasted_iota(jnp.int32, (1, LANES), 1) >= C
+    squares = jnp.where(spare, count, jnp.sum(squares, axis=0, keepdims=True))
+    both = jnp.concatenate([average, squares], axis=0)
+    stats[...] = jnp.broadcast_to(both[None], (DEVICES, 2, LANES))
+
+
+def last_kernel(live, conved, stats, gain, shift, out):
     step = pl.program_id(0)
-    average, spread = moments(stats, counts[...])
+    average, spread = moments(stats)
     factor = gain[...] * lax.rsqrt(spread + NORM_EPS)
     size = conved.shape[0]
     row = lax.broadcasted_iota(jnp.int32, (size, LANES), 0) + step * size
@@ -245,19 +252,19 @@
     )(picks, own)
 
 
-def next_send(picks, live, conved, stats, counts, gain, shift):
+def next_send(picks, live, conved, stats, gain, shift):
     return pl.pallas_call(
         next_send_kernel,
-        in_specs=[IN_ANY, IN_SMEM] + [IN_VMEM] * 5,
+        in_specs=[IN_ANY, IN_SMEM] + [IN_VMEM] * 4,
         out_specs=[IN_VMEM, IN_VMEM],
         out_shape=[
             jax.ShapeDtypeStruct((DEVICES, C, LANES), BF16),
-            jax.ShapeDtypeStruct((V_DEV, LANES), BF16),
+            jax.ShapeDtypeStruct((V_DEV, C), BF16),
         ],
         scratch_shapes=send_scratch(),
         compiler_params=params(),
         name="next_send",
-    )(picks, live, conved, stats, counts, gain, shift)
+    )(picks, live, conved, stats, gain, shift)
 
 
 @jax.jit
@@ -268,7 +275,7 @@
         out_specs=[IN_VMEM, IN_VMEM],
         out_shape=[
             jax.ShapeDtypeStruct((V_DEV, LANES), F32),
-            jax.ShapeDtypeStruct((2, LANES), F32),
+            jax.ShapeDtypeStruct((DEVICES, 2, LANES), F32),
         ],
         scratch_shapes=[
             pltpu.VMEM((MISSING + 8, LANES), F32),
@@ -282,8 +289,8 @@
     )(live, maps, own, arrived, weight, middle)
 
 
-def last_norm(live, conved, stats, counts, gain, shift):
-    size = 1024
+def last_norm(live, conved, stats, gain, shift):
+    size = 2048
     whole = lambda *dims: pl.BlockSpec(dims, lambda i: (0,) * len(dims))
     return pl.pallas_call(
         last_kernel,
@@ -292,7 +299,6 @@
             IN_SMEM,
             pl.BlockSpec((size, LANES), lambda i: (i, 0)),
             whole(DEVICES, 2, LANES),
-            whole(DEVICES, LANES),
             whole(1, LANES),
             whole(1, LANES),
         ],
@@ -300,15 +306,11 @@
         out_shape=jax.ShapeDtypeStruct((C, V_DEV), BF16),
         compiler_params=params(),
         name="last_norm",
-    )(live, conved, stats, counts, gain, shift)
+    )(live, conved, stats, gain, shift)
 
 
 def exchange(parcels):
     return lax.all_to_all(parcels, AXES, split_axis=0, concat_axis=0, tiled=True)
-
-
-def share(stats):
-    return exchange(jnp.broadcast_to(stats[None], (DEVICES, 2, LANES)))
 
 
 def prepare_weight(weight):
@@ -321,20 +323,19 @@
 ):
     device = lax.axis_index(AXES)
     live = lax.dynamic_slice_in_dim(active_rows, device, 1)
-    counts = jnp.broadcast_to(active_rows.astype(F32)[:, None], (DEVICES, LANES))
     gain = jnp.pad(norm_gain, ((0, 0), (0, LANES - C)))
     shift = jnp.pad(norm_shift, ((0, 0), (0, LANES - C)))
     picks = send_rows.reshape(DEVICES // GROUP, GROUP, CAP)
 
-    own = jnp.pad(jnp.transpose(features), ((0, 0), (0, LANES - C)))
+    own = jnp.transpose(features)
     arrived = exchange(first_send(picks, own))
     conved, stats = convolve(live, neighbors, own, arrived, *prepare_weight(weight_one))
-    stats = share(stats)
-    parcels, own = next_send(picks, live, conved, stats, counts, gain[0:1], shift[0:1])
+    stats = exchange(stats)
+    parcels, own = next_send(picks, live, conved, stats, gain[0:1], shift[0:1])
     arrived = exchange(parcels)
     conved, stats = convolve(live, neighbors, own, arrived, *prepare_weight(weight_two))
-    stats = share(stats)
-    return last_norm(live, conved, stats, counts, gain[1:2], shift[1:2])
+    stats = exchange(stats)
+    return last_norm(live, conved, stats, gain[1:2], shift[1:2])
 
 
 def solution(mesh):

time: 479 us -> 458 us (0.956)
  Pallas kernels: 184 us -> 119 us
  blocking collectives: 93.1 us -> 117 us
  starting transfers between devices: 98.9 us -> 122 us
    pallas_call x2, Pallas kernels: 147 us -> 84.5 us  [convolve(): pl.pallas_call(conv_kernel, in_specs=[IN_SMEM, IN_ANY] + [IN_VMEM] * 4, o...]
    all_to_all x1, blocking collectives: 93.1 us -> 117 us  [exchange(): lax.all_to_all(parcels, AXES, split_axis=0, concat_axis=0, tiled=True)]
    all_to_all x3, starting transfers between devices: 98.9 us -> 122 us  [exchange(): lax.all_to_all(parcels, AXES, split_axis=0, concat_axis=0, tiled=True)]
where the time goes in v3:
time: 458 us
  starting transfers between devices  122 us (27%)
  Pallas kernels  119 us (26%)
  blocking collectives  117 us (26%)
  waiting for transfers between devices  83.5 us (18%)
  local copies, waits for them, and re-layouts  14.4 us (3%)
    all_to_all x3, starting transfers between devices, exchange(): lax.all_to_all(parcels, AXES, split_axis=0, concat_axis=0, tiled=True)  122 us
    all_to_all x1, blocking collectives, exchange(): lax.all_to_all(parcels, AXES, split_axis=0, concat_axis=0, tiled=True)  117 us
    pallas_call x2, Pallas kernels, convolve(): pl.pallas_call(conv_kernel, in_specs=[IN_SMEM, IN_ANY] + [IN_VMEM] * 4, o...  84.5 us
    all_to_all x3, waiting for transfers between devices, exchange(): lax.all_to_all(parcels, AXES, split_axis=0, concat_axis=0, tiled=True)  83.5 us
    pallas_call x1, Pallas kernels, next_send(): pl.pallas_call(next_send_kernel, in_specs=[IN_ANY, IN_SMEM] + [IN_VMEM] *...  15.4 us
    pallas_call x1, Pallas kernels, first_send(): pl.pallas_call(first_send_kernel, in_specs=[IN_ANY, IN_VMEM], out_specs=I...  13.3 us
  transfers between devices with their start and end apart: 3, of which 3 were waited for; matrix products, arithmetic and copies ran while one was open for 2% of the time, Pallas kernels for 0%

profile of v3, /device:TPU:1, one launch (start us, length us, event | category | flops | bytes accessed | tf_op | source)
XLA Modules:
  0.0 457.7 jit_solution(3773706214892318715)
XLA Ops:
  0.0 3.9 copy.9
  3.9 13.3 %first_send.1 = bf16[128,96,128]{2,1,0:T(8,128)(2,1)} custom-call(s32[16,8,128]{2,1,0:T(8,128)} %bitcast.8, bf16[8192,96]{1,0:T(8,128)(2,1)} %bitcast.6), custom_call_target="tpu_custom_call" | custom-call | tf_op jit(solution)/shard_map/first_send/pallas_call | solution.py:244
  17.1 0.0 copy-start.5
  17.2 11.5 %all-to-all-start = ((bf16[128,96,128]{2,1,0:T(8,128)(2,1)}), bf16[128,96,128]{2,1,0:T(8,128)(2,1)S(1)}, u32[]{:S(2)}, u32[]{:S(2)}) async-start(bf16[128,96,128]{2,1,0:T(8,128)(2,1)} %first_send.1), calls=%async_computation | async-start | bytes 6291456 | tf_op jit(solution)/shard_map/all_to_all | solution.py:313
  28.7 0.0 copy-done.5
  28.7 0.6 dynamic_slice.3.live
  29.3 1.3 fusion.middle
  30.6 1.3 pad_slice_fusion.5
  31.9 1.0 pad_maximum_fusion.weight
  32.9 0.0 copy-start.4
  32.9 36.7 %all-to-all-done.arrived = bf16[128,96,128]{2,1,0:T(8,128)(2,1)S(1)} async-done(((bf16[128,96,128]{2,1,0:T(8,128)(2,1)}), bf16[128,96,128]{2,1,0:T(8,128)(2,1)S(1)}, u32[]{:S(2)}, u32[]{:S(2)}) %all-to-all-start) | async-done | bytes 3145760 | tf_op jit(solution)/shard_map/all_to_all | solution.py:313
  69.6 0.0 copy-start
  69.6 1.7 copy-done
  71.3 42.2 %sparse_conv.2 = (f32[8192,128]{1,0:T(8,128)}, f32[128,2,128]{2,1,0:T(2,128)}) custom-call(s32[1]{0:T(128)} %dynamic_slice.3.live, s32[27,8192]{1,0:T(8,128)} %maps.3, bf16[8192,96]{1,0:T(8,128)(2,1)} %bitcast.7, bf16[128,96,128]{2,1,0:T(8,128)(2,1)} %copy-done, bf16[13,256,128]{2,1,0:T(8,128)(2,1)} %pad_maximum_fusion.weight, bf16[128,128]{1,0:T(8,128)(2,1)} %fusion.middle), custom_call_target="tpu_custom_call" | custom-call | tf_op jit(solution)/shard_map/jit(convolve)/sparse_conv/pallas_call | solution.py:272
  113.5 106.3 %all-to-all-start.1 = ((f32[128,2,128]{2,1,0:T(2,128)}), f32[128,2,128]{2,1,0:T(2,128)S(1)}, u32[]{:S(2)}, u32[]{:S(2)}) async-start(f32[128,2,128]{2,1,0:T(2,128)} %get-tuple-element.12), calls=%async_computation.1 | async-start | bytes 262144 | tf_op jit(solution)/shard_map/all_to_all | solution.py:313
  219.9 0.0 copy-done.3
  219.9 0.0 copy-done.4
  219.9 0.6 pad_slice_fusion.6
  220.5 9.4 %all-to-all-done.1.stats = f32[128,2,128]{2,1,0:T(2,128)S(1)} async-done(((f32[128,2,128]{2,1,0:T(2,128)}), f32[128,2,128]{2,1,0:T(2,128)S(1)}, u32[]{:S(2)}, u32[]{:S(2)}) %all-to-all-start.1) | async-done | bytes 131104 | tf_op jit(solution)/shard_map/all_to_all | solution.py:313
  229.9 0.0 copy-start.2
  229.9 0.7 copy-done.2
  230.6 15.4 %next_send.1 = (bf16[128,96,128]{2,1,0:T(8,128)(2,1)}, bf16[8192,96]{1,0:T(8,128)(2,1)}) custom-call(s32[16,8,128]{2,1,0:T(8,128)} %bitcast.9, s32[1]{0:T(128)} %dynamic_slice.3.live, f32[8192,128]{1,0:T(8,128)} %get-tuple-element.11.conved, f32[128,2,128]{2,1,0:T(2,128)} %copy-done.2, f32[1,128]{1,0:T(1,128)} %get-tuple-element.25.gain, ...), custom_call_target="tpu_custom_call" | custom-call | tf_op jit(solution)/shard_map/next_send/pallas_call | solution.py:256
  246.0 4.2 all-to-all-start.2
  250.2 1.4 fusion.1.middle
  251.6 1.3 pad_slice_fusion.2
  252.8 1.0 pad_maximum_fusion.1.weight
  253.8 37.3 %all-to-all-done.2.arrived = bf16[128,96,128]{2,1,0:T(8,128)(2,1)S(1)} async-done(((bf16[128,96,128]{2,1,0:T(8,128)(2,1)}), bf16[128,96,128]{2,1,0:T(8,128)(2,1)S(1)}, u32[]{:S(2)}, u32[]{:S(2)}) %all-to-all-start.2) | async-done | bytes 3145760 | tf_op jit(solution)/shard_map/all_to_all | solution.py:313
  291.1 0.0 copy-start.1
  291.1 1.7 copy-done.1
  292.8 42.2 %sparse_conv.3 = (f32[8192,128]{1,0:T(8,128)}, f32[128,2,128]{2,1,0:T(2,128)}) custom-call(s32[1]{0:T(128)} %dynamic_slice.3.live, s32[27,8192]{1,0:T(8,128)} %maps.3, bf16[8192,96]{1,0:T(8,128)(2,1)} %get-tuple-element.13.own, bf16[128,96,128]{2,1,0:T(8,128)(2,1)} %copy-done.1, bf16[13,256,128]{2,1,0:T(8,128)(2,1)} %pad_maximum_fusion.1.weight, ...), custom_call_target="tpu_custom_call" | custom-call | tf_op jit(solution)/shard_map/jit(convolve)/sparse_conv/pallas_call | solution.py:272
  335.1 116.8 %all_to_all.20.stats = f32[128,2,128]{2,1,0:T(2,128)} all-to-all(f32[128,2,128]{2,1,0:T(2,128)} %get-tuple-element.16), channel_id=1, replica_groups=mesh['region'=8,'sub'=16] {'region','sub'}, dimensions={0} | all-to-all | bytes 262144 | tf_op jit(solution)/shard_map/all_to_all | solution.py:313
  451.9 5.8 %last_norm.1 = bf16[96,8192]{1,0:T(8,128)(2,1)} custom-call(s32[1]{0:T(128)} %dynamic_slice.3.live, f32[8192,128]{1,0:T(8,128)} %get-tuple-element.15.conved, f32[128,2,128]{2,1,0:T(2,128)} %all_to_all.20.stats, f32[1,128]{1,0:T(1,128)} %get-tuple-element.26.gain, f32[1,128]{1,0:T(1,128)} %get-tuple-element.21.shift), custom_call_target="tpu_custom_call" | custom-call | tf_op jit(solution)/shard_map/last_norm/pallas_call | solution.py:295
  (1 shorter events, 0.0 us)
Async XLA Ops:
  17.1 11.5 %copy-start.5 = (s32[128]{0:T(128)S(1)}, s32[128]{0:T(128)}, u32[]{:S(2)}) copy-start(s32[128]{0:T(128)} %param.11) | copy-start | bytes 1540
  17.2 52.4 %all-to-all-start = ((bf16[128,96,128]{2,1,0:T(8,128)(2,1)}), bf16[128,96,128]{2,1,0:T(8,128)(2,1)S(1)}, u32[]{:S(2)}, u32[]{:S(2)}) async-start(bf16[128,96,128]{2,1,0:T(8,128)(2,1)} %first_send.1), calls=%async_computation | async-start | bytes 6291456 | tf_op jit(solution)/shard_map/all_to_all | solution.py:313
  32.9 187.0 %copy-start.3 = (f32[2,96]{1,0:T(2,128)S(1)}, f32[2,96]{1,0:T(2,128)}, u32[]{:S(2)}) copy-start(f32[2,96]{1,0:T(2,128)} %param.15) | copy-start | bytes 2308
  32.9 187.0 %copy-start.4 = (f32[2,96]{1,0:T(2,128)S(1)}, f32[2,96]{1,0:T(2,128)}, u32[]{:S(2)}) copy-start(f32[2,96]{1,0:T(2,128)} %param.14) | copy-start | bytes 2308
  69.6 1.7 copy-start
  113.5 116.4 %all-to-all-start.1 = ((f32[128,2,128]{2,1,0:T(2,128)}), f32[128,2,128]{2,1,0:T(2,128)S(1)}, u32[]{:S(2)}, u32[]{:S(2)}) async-start(f32[128,2,128]{2,1,0:T(2,128)} %get-tuple-element.12), calls=%async_computation.1 | async-start | bytes 262144 | tf_op jit(solution)/shard_map/all_to_all | solution.py:313
  229.9 0.7 copy-start.2
  246.0 45.1 %all-to-all-start.2 = ((bf16[128,96,128]{2,1,0:T(8,128)(2,1)}), bf16[128,96,128]{2,1,0:T(8,128)(2,1)S(1)}, u32[]{:S(2)}, u32[]{:S(2)}) async-start(bf16[128,96,128]{2,1,0:T(8,128)(2,1)} %get-tuple-element.14), calls=%async_computation.2 | async-start | bytes 6291456 | tf_op jit(solution)/shard_map/all_to_all | solution.py:313
  291.1 1.7 copy-start.1

commit v4 on v3

--- a/solution.py
+++ b/solution.py
@@ -16,6 +16,7 @@
 LANES = 128
 V_DEV = 8192
 CAP = 128
+PART = 32
 GROUP = 8
 SLOTS = 4
 DEVICES = 128
@@ -127,11 +128,19 @@
     send_rows_packed(picks, table, stage, out, index, sems)
 
 
-def conv_kernel(live, maps, own, arrived, weight, middle, out, stats, table, stage, sums, index, sems):
+def conv_kernel(
+    live, maps, own, parcels, weight, middle, out, stats, table, stage, sums, arrived, index, sems, parts
+):
     def fetch(block, slot):
         columns = pl.ds(pl.multiple_of(block * BLOCK, BLOCK), BLOCK)
         return pltpu.make_async_copy(maps.at[:, columns], index.at[slot], sems.at[slot])
 
+    def receive(part):
+        peers = pl.ds(part * PART, PART)
+        return pltpu.make_async_copy(parcels.at[peers], arrived.at[peers], parts.at[part])
+
+    for part in range(DEVICES // PART):
+        receive(part).start()
     fetch(0, 0).start()
     blocks = live[0] // BLOCK
     lane = lax.broadcasted_iota(jnp.int32, (TAIL, LANES), 1)
@@ -153,7 +162,9 @@
         return carry
 
     lax.fori_loop(0, V_DEV // BLOCK, fill_own, 0, unroll=2)
-    lax.fori_loop(0, DEVICES, fill_arrived, 0, unroll=8)
+    for part in range(DEVICES // PART):
+        receive(part).wait()
+        lax.fori_loop(part * PART, (part + 1) * PART, fill_arrived, 0, unroll=8)
     table[MISSING : MISSING + 8, :] = jnp.zeros((8, LANES), F32)
 
     def multiply(slot, p):
@@ -216,15 +227,21 @@
     stats[...] = jnp.broadcast_to(both[None], (DEVICES, 2, LANES))
 
 
-def last_kernel(live, conved, stats, gain, shift, out):
-    step = pl.program_id(0)
+def turn_kernel(conved, out):
+    out[...] = jnp.transpose(conved[...])[0:C, :]
+
+
+def last_kernel(live, turned, stats, gain, shift, out):
     average, spread = moments(stats)
     factor = gain[...] * lax.rsqrt(spread + NORM_EPS)
-    size = conved.shape[0]
-    row = lax.broadcasted_iota(jnp.int32, (size, LANES), 0) + step * size
-    normed = jnp.maximum((conved[...] - average) * factor + shift[...], 0.0)
-    normed = jnp.where(row < live[0], normed, 0.0)
-    out[...] = jnp.transpose(normed)[0:C, :].astype(BF16)
+
+    def upright(row):
+        return jnp.transpose(jnp.broadcast_to(row, (LANES, LANES)))[0:C, 0:1]
+
+    size = turned.shape[1]
+    column = lax.broadcasted_iota(jnp.int32, (C, size), 1) + pl.program_id(0) * size
+    normed = (turned[...] - upright(average)) * upright(factor) + upright(shift[...])
+    out[...] = jnp.where(column < live[0], jnp.maximum(normed, 0.0), 0.0).astype(BF16)
 
 
 def params():
@@ -271,7 +288,7 @@
 def convolve(live, maps, own, arrived, weight, middle):
     return pl.pallas_call(
         conv_kernel,
-        in_specs=[IN_SMEM, IN_ANY] + [IN_VMEM] * 4,
+        in_specs=[IN_SMEM, IN_ANY, IN_VMEM, IN_ANY, IN_VMEM, IN_VMEM],
         out_specs=[IN_VMEM, IN_VMEM],
         out_shape=[
             jax.ShapeDtypeStruct((V_DEV, LANES), F32),
@@ -281,23 +298,41 @@
             pltpu.VMEM((MISSING + 8, LANES), F32),
             pltpu.VMEM((2, PAIRS, BLOCK, 2 * LANES), F32),
             pltpu.VMEM((8, LANES), F32),
+            pltpu.VMEM((DEVICES, C, LANES), BF16),
             pltpu.SMEM((2, K3, BLOCK), jnp.int32),
             pltpu.SemaphoreType.DMA((2,)),
+            pltpu.SemaphoreType.DMA((DEVICES // PART,)),
         ],
         compiler_params=params(),
         name="sparse_conv",
     )(live, maps, own, arrived, weight, middle)
 
 
-def last_norm(live, conved, stats, gain, shift):
-    size = 2048
+def turn(conved):
+    size = 1024
+    return pl.pallas_call(
+        turn_kernel,
+        grid=(V_DEV // size,),
+        in_specs=[pl.BlockSpec((size, LANES), lambda i: (i, 0))],
+        out_specs=pl.BlockSpec((C, size), lambda i: (0, i)),
+        out_shape=jax.ShapeDtypeStruct((C, V_DEV), F32),
+        compiler_params=params(),
+        cost_estimate=pl.CostEstimate(
+            flops=V_DEV * LANES, bytes_accessed=V_DEV * (LANES + C) * 4, transcendentals=0
+        ),
+        name="turn",
+    )(conved)
+
+
+def last_norm(live, turned, stats, gain, shift):
+    size = 4096
     whole = lambda *dims: pl.BlockSpec(dims, lambda i: (0,) * len(dims))
     return pl.pallas_call(
         last_kernel,
         grid=(V_DEV // size,),
         in_specs=[
             IN_SMEM,
-            pl.BlockSpec((size, LANES), lambda i: (i, 0)),
+            pl.BlockSpec((C, size), lambda i: (0, i)),
             whole(DEVICES, 2, LANES),
             whole(1, LANES),
             whole(1, LANES),
@@ -306,7 +341,7 @@
         out_shape=jax.ShapeDtypeStruct((C, V_DEV), BF16),
         compiler_params=params(),
         name="last_norm",
-    )(live, conved, stats, gain, shift)
+    )(live, turned, stats, gain, shift)
 
 
 def exchange(parcels):
@@ -335,7 +370,7 @@
     arrived = exchange(parcels)
     conved, stats = convolve(live, neighbors, own, arrived, *prepare_weight(weight_two))
     stats = exchange(stats)
-    return last_norm(live, conved, stats, gain[1:2], shift[1:2])
+    return last_norm(live, turn(conved), stats, gain[1:2], shift[1:2])
 
 
 def solution(mesh):

time: 458 us -> 458 us (level)
  Pallas kernels: 119 us -> 261 us
  blocking collectives: 117 us -> 0 us
  starting transfers between devices: 122 us -> 92 us
    pallas_call x2 -> x3, Pallas kernels: 84.5 us -> 228 us  [the longest x2 221 us: convolve(): pl.pallas_call(conv_kernel, in_specs=[IN_SMEM, IN_ANY, IN_VMEM, IN_ANY, I...]
    all_to_all x1 -> x0, blocking collectives: 117 us -> none  [exchange(): lax.all_to_all(parcels, AXES, split_axis=0, concat_axis=0, tiled=True)]
    all_to_all x3 -> x4, starting transfers between devices: 122 us -> 92 us  [exchange(): lax.all_to_all(parcels, AXES, split_axis=0, concat_axis=0, tiled=True)]
    all_to_all x3 -> x4, waiting for transfers between devices: 83.5 us -> 86.8 us  [exchange(): lax.all_to_all(parcels, AXES, split_axis=0, concat_axis=0, tiled=True)]
  transfers between devices with their start and end apart: 3 -> 4, of which waited for: 3 -> 4; matrix products, arithmetic and copies ran while one was open for 2% -> 2% of each run, Pallas kernels for 0% -> 2%
where the time goes in v4:
time: 458 us; the launch traced here: 457 us
  Pallas kernels  261 us (57%)
  starting transfers between devices  92 us (20%)
  waiting for transfers between devices  86.8 us (19%)
  local copies, waits for them, and re-layouts  15 us (3%)
    pallas_call x2, Pallas kernels, convolve(): pl.pallas_call(conv_kernel, in_specs=[IN_SMEM, IN_ANY, IN_VMEM, IN_ANY, I...  221 us
    all_to_all x4, starting transfers between devices, exchange(): lax.all_to_all(parcels, AXES, split_axis=0, concat_axis=0, tiled=True)  92 us
    all_to_all x4, waiting for transfers between devices, exchange(): lax.all_to_all(parcels, AXES, split_axis=0, concat_axis=0, tiled=True)  86.8 us
    pallas_call x1, Pallas kernels, next_send(): pl.pallas_call(next_send_kernel, in_specs=[IN_ANY, IN_SMEM] + [IN_VMEM] *...  15.9 us
    pallas_call x1, Pallas kernels, first_send(): pl.pallas_call(first_send_kernel, in_specs=[IN_ANY, IN_VMEM], out_specs=I...  13.3 us
  transfers between devices with their start and end apart: 4, of which 4 were waited for; matrix products, arithmetic and copies ran while one was open for 2% of the time, Pallas kernels for 2%

profile of v4, /device:TPU:1, one launch (start us, length us, event | category | flops | bytes accessed | tf_op | source)
XLA Modules:
  0.0 457.3 jit_solution(7340925794949264190)
XLA Ops:
  0.0 3.9 copy.9
  3.9 13.3 %first_send.1 = bf16[128,96,128]{2,1,0:T(8,128)(2,1)} custom-call(s32[16,8,128]{2,1,0:T(8,128)} %bitcast.8, bf16[8192,96]{1,0:T(8,128)(2,1)} %bitcast.6), custom_call_target="tpu_custom_call" | custom-call | tf_op jit(solution)/shard_map/first_send/pallas_call | solution.py:261
  17.1 0.0 copy-start.6
  17.2 11.5 %all-to-all-start = ((bf16[128,96,128]{2,1,0:T(8,128)(2,1)}), bf16[128,96,128]{2,1,0:T(8,128)(2,1)S(1)}, u32[]{:S(2)}, u32[]{:S(2)}) async-start(bf16[128,96,128]{2,1,0:T(8,128)(2,1)} %first_send.1), calls=%async_computation | async-start | bytes 6291456 | tf_op jit(solution)/shard_map/all_to_all | solution.py:348
  28.7 0.0 copy-done.6
  28.7 0.6 dynamic_slice.3.live
  29.3 1.4 fusion.middle
  30.7 1.3 pad_slice_fusion.5
  31.9 1.0 pad_maximum_fusion.weight
  32.9 0.0 copy-start.4
  32.9 36.7 %all-to-all-done.parcels = bf16[128,96,128]{2,1,0:T(8,128)(2,1)S(1)} async-done(((bf16[128,96,128]{2,1,0:T(8,128)(2,1)}), bf16[128,96,128]{2,1,0:T(8,128)(2,1)S(1)}, u32[]{:S(2)}, u32[]{:S(2)}) %all-to-all-start) | async-done | bytes 3145760 | tf_op jit(solution)/shard_map/all_to_all | solution.py:348
  69.6 1.7 copy-done
  71.2 110.3 %sparse_conv.2 = (f32[8192,128]{1,0:T(8,128)}, f32[128,2,128]{2,1,0:T(2,128)}) custom-call(s32[1]{0:T(128)} %dynamic_slice.3.live, s32[27,8192]{1,0:T(8,128)} %maps.3, bf16[8192,96]{1,0:T(8,128)(2,1)} %bitcast.7, bf16[128,96,128]{2,1,0:T(8,128)(2,1)} %copy-done, bf16[13,256,128]{2,1,0:T(8,128)(2,1)} %pad_maximum_fusion.weight, bf16[128,128]{1,0:T(8,128)(2,1)} %fusion.middle), custom_call_target="tpu_custom_call" | custom-call | tf_op jit(solution)/shard_map/jit(convolve)/sparse_conv/pallas_call | solution.py:289
  181.6 38.1 %all-to-all-start.1 = ((f32[128,2,128]{2,1,0:T(2,128)}), f32[128,2,128]{2,1,0:T(2,128)S(1)}, u32[]{:S(2)}, u32[]{:S(2)}) async-start(f32[128,2,128]{2,1,0:T(2,128)} %get-tuple-element.12), calls=%async_computation.1 | async-start | bytes 262144 | tf_op jit(solution)/shard_map/all_to_all | solution.py:348
  219.7 0.0 copy-done.4
  219.7 0.0 copy-done.5
  219.7 0.6 pad_slice_fusion.6
  220.3 9.6 %all-to-all-done.1.stats = f32[128,2,128]{2,1,0:T(2,128)S(1)} async-done(((f32[128,2,128]{2,1,0:T(2,128)}), f32[128,2,128]{2,1,0:T(2,128)S(1)}, u32[]{:S(2)}, u32[]{:S(2)}) %all-to-all-start.1) | async-done | bytes 131104 | tf_op jit(solution)/shard_map/all_to_all | solution.py:348
  229.9 0.7 copy-done.2
  230.5 15.9 %next_send.1 = (bf16[128,96,128]{2,1,0:T(8,128)(2,1)}, bf16[8192,96]{1,0:T(8,128)(2,1)}) custom-call(s32[16,8,128]{2,1,0:T(8,128)} %bitcast.9, s32[1]{0:T(128)} %dynamic_slice.3.live, f32[8192,128]{1,0:T(8,128)} %get-tuple-element.11.conved, f32[128,2,128]{2,1,0:T(2,128)} %copy-done.2, f32[1,128]{1,0:T(1,128)} %get-tuple-element.25.gain, ...), custom_call_target="tpu_custom_call" | custom-call | tf_op jit(solution)/shard_map/next_send/pallas_call | solution.py:273
  246.4 4.3 all-to-all-start.2
  250.7 1.4 fusion.1.middle
  252.1 1.3 pad_slice_fusion.2
  253.4 1.0 pad_maximum_fusion.1.weight
  254.3 37.4 %all-to-all-done.2.parcels = bf16[128,96,128]{2,1,0:T(8,128)(2,1)S(1)} async-done(((bf16[128,96,128]{2,1,0:T(8,128)(2,1)}), bf16[128,96,128]{2,1,0:T(8,128)(2,1)S(1)}, u32[]{:S(2)}, u32[]{:S(2)}) %all-to-all-start.2) | async-done | bytes 3145760 | tf_op jit(solution)/shard_map/all_to_all | solution.py:348
  291.8 1.7 copy-done.1
  293.4 110.3 %sparse_conv.3 = (f32[8192,128]{1,0:T(8,128)}, f32[128,2,128]{2,1,0:T(2,128)}) custom-call(s32[1]{0:T(128)} %dynamic_slice.3.live, s32[27,8192]{1,0:T(8,128)} %maps.3, bf16[8192,96]{1,0:T(8,128)(2,1)} %get-tuple-element.13.own, bf16[128,96,128]{2,1,0:T(8,128)(2,1)} %copy-done.1, bf16[13,256,128]{2,1,0:T(8,128)(2,1)} %pad_maximum_fusion.1.weight, ...), custom_call_target="tpu_custom_call" | custom-call | tf_op jit(solution)/shard_map/jit(convolve)/sparse_conv/pallas_call | solution.py:289
  403.8 38.1 %all-to-all-start.3 = ((f32[128,2,128]{2,1,0:T(2,128)}), f32[128,2,128]{2,1,0:T(2,128)S(1)}, u32[]{:S(2)}, u32[]{:S(2)}) async-start(f32[128,2,128]{2,1,0:T(2,128)} %get-tuple-element.16), calls=%async_computation.3 | async-start | bytes 262144 | tf_op jit(solution)/shard_map/all_to_all | solution.py:348
  441.9 7.0 %turn.1.turned = f32[96,8192]{1,0:T(8,128)} custom-call(f32[8192,128]{1,0:T(8,128)} %get-tuple-element.15.conved), custom_call_target="tpu_custom_call" | custom-call | flops 1048576 | bytes 7340032 | tf_op jit(solution)/shard_map/turn/pallas_call | solution.py:313
  448.9 3.2 all-to-all-done.3.stats
  452.1 0.6 copy-done.3
  452.7 4.6 %last_norm.1 = bf16[96,8192]{1,0:T(8,128)(2,1)} custom-call(s32[1]{0:T(128)} %dynamic_slice.3.live, f32[96,8192]{1,0:T(8,128)} %turn.1.turned, f32[128,2,128]{2,1,0:T(2,128)} %copy-done.3, f32[1,128]{1,0:T(1,128)} %get-tuple-element.26.gain, f32[1,128]{1,0:T(1,128)} %get-tuple-element.21.shift), custom_call_target="tpu_custom_call" | custom-call | tf_op jit(solution)/shard_map/last_norm/pallas_call | solution.py:330
  (5 shorter events, 0.0 us)
Async XLA Ops:
  17.1 11.5 %copy-start.6 = (s32[128]{0:T(128)S(1)}, s32[128]{0:T(128)}, u32[]{:S(2)}) copy-start(s32[128]{0:T(128)} %param.11) | copy-start | bytes 1540
  17.2 52.4 %all-to-all-start = ((bf16[128,96,128]{2,1,0:T(8,128)(2,1)}), bf16[128,96,128]{2,1,0:T(8,128)(2,1)S(1)}, u32[]{:S(2)}, u32[]{:S(2)}) async-start(bf16[128,96,128]{2,1,0:T(8,128)(2,1)} %first_send.1), calls=%async_computation | async-start | bytes 6291456 | tf_op jit(solution)/shard_map/all_to_all | solution.py:348
  32.9 186.8 %copy-start.4 = (f32[2,96]{1,0:T(2,128)S(1)}, f32[2,96]{1,0:T(2,128)}, u32[]{:S(2)}) copy-start(f32[2,96]{1,0:T(2,128)} %param.15) | copy-start | bytes 2308
  32.9 186.8 %copy-start.5 = (f32[2,96]{1,0:T(2,128)S(1)}, f32[2,96]{1,0:T(2,128)}, u32[]{:S(2)}) copy-start(f32[2,96]{1,0:T(2,128)} %param.14) | copy-start | bytes 2308
  69.6 1.7 copy-start
  181.6 48.3 %all-to-all-start.1 = ((f32[128,2,128]{2,1,0:T(2,128)}), f32[128,2,128]{2,1,0:T(2,128)S(1)}, u32[]{:S(2)}, u32[]{:S(2)}) async-start(f32[128,2,128]{2,1,0:T(2,128)} %get-tuple-element.12), calls=%async_computation.1 | async-start | bytes 262144 | tf_op jit(solution)/shard_map/all_to_all | solution.py:348
  229.9 0.7 copy-start.2
  246.4 45.3 %all-to-all-start.2 = ((bf16[128,96,128]{2,1,0:T(8,128)(2,1)}), bf16[128,96,128]{2,1,0:T(8,128)(2,1)S(1)}, u32[]{:S(2)}, u32[]{:S(2)}) async-start(bf16[128,96,128]{2,1,0:T(8,128)(2,1)} %get-tuple-element.14), calls=%async_computation.2 | async-start | bytes 6291456 | tf_op jit(solution)/shard_map/all_to_all | solution.py:348
  291.8 1.7 copy-start.1
  403.8 48.3 %all-to-all-start.3 = ((f32[128,2,128]{2,1,0:T(2,128)}), f32[128,2,128]{2,1,0:T(2,128)S(1)}, u32[]{:S(2)}, u32[]{:S(2)}) async-start(f32[128,2,128]{2,1,0:T(2,128)} %get-tuple-element.16), calls=%async_computation.3 | async-start | bytes 262144 | tf_op jit(solution)/shard_map/all_to_all | solution.py:348
  452.1 0.6 copy-start.3

commit v5 on v4

--- a/solution.py
+++ b/solution.py
@@ -97,7 +97,7 @@
         table[rows, :] = widen(own[rows, :].astype(F32))
         return carry
 
-    lax.fori_loop(0, V_DEV // BLOCK, fill, 0)
+    lax.fori_loop(0, V_DEV // BLOCK, fill, 0, unroll=4)
     send_rows_packed(picks, table, stage, out, index, sems)
 
 
@@ -129,7 +129,7 @@
 
 
 def conv_kernel(
-    live, maps, own, parcels, weight, middle, out, stats, table, stage, sums, arrived, index, sems, parts
+    live, maps, own, parcels, weight, middle, result, stats, table, stage, sums, out, arrived, index, sems, parts, away
 ):
     def fetch(block, slot):
         columns = pl.ds(pl.multiple_of(block * BLOCK, BLOCK), BLOCK)
@@ -212,6 +212,8 @@
         total = total + multiply(last % 2, p)
     sums[...] += finish(last, total)
 
+    leave = pltpu.make_async_copy(out, result, away)
+    leave.start()
     count = (blocks * BLOCK).astype(F32)
     average = jnp.sum(sums[...], axis=0, keepdims=True) / count
 
@@ -225,6 +227,7 @@
     squares = jnp.where(spare, count, jnp.sum(squares, axis=0, keepdims=True))
     both = jnp.concatenate([average, squares], axis=0)
     stats[...] = jnp.broadcast_to(both[None], (DEVICES, 2, LANES))
+    leave.wait()
 
 
 def turn_kernel(conved, out):
@@ -289,7 +292,7 @@
     return pl.pallas_call(
         conv_kernel,
         in_specs=[IN_SMEM, IN_ANY, IN_VMEM, IN_ANY, IN_VMEM, IN_VMEM],
-        out_specs=[IN_VMEM, IN_VMEM],
+        out_specs=[IN_ANY, IN_VMEM],
         out_shape=[
             jax.ShapeDtypeStruct((V_DEV, LANES), F32),
             jax.ShapeDtypeStruct((DEVICES, 2, LANES), F32),
@@ -298,10 +301,12 @@
             pltpu.VMEM((MISSING + 8, LANES), F32),
             pltpu.VMEM((2, PAIRS, BLOCK, 2 * LANES), F32),
             pltpu.VMEM((8, LANES), F32),
+            pltpu.VMEM((V_DEV, LANES), F32),
             pltpu.VMEM((DEVICES, C, LANES), BF16),
             pltpu.SMEM((2, K3, BLOCK), jnp.int32),
             pltpu.SemaphoreType.DMA((2,)),
             pltpu.SemaphoreType.DMA((DEVICES // PART,)),
+            pltpu.SemaphoreType.DMA,
         ],
         compiler_params=params(),
         name="sparse_conv",

time: 458 us -> 453 us (0.989)
  Pallas kernels: 261 us -> 125 us
  starting transfers between devices: 92 us -> 222 us
    pallas_call x2, Pallas kernels: 221 us -> 84.9 us  [convolve(): pl.pallas_call(conv_kernel, in_specs=[IN_SMEM, IN_ANY, IN_VMEM, IN_ANY, I...]
    all_to_all x4, starting transfers between devices: 92 us -> 222 us  [exchange(): lax.all_to_all(parcels, AXES, split_axis=0, concat_axis=0, tiled=True)]
where the time goes in v5:
time: 453 us; the launch traced here: 451 us
  starting transfers between devices  222 us (49%)
  Pallas kernels  125 us (28%)
  waiting for transfers between devices  86.5 us (19%)
  local copies, waits for them, and re-layouts  15 us (3%)
    all_to_all x4, starting transfers between devices, exchange(): lax.all_to_all(parcels, AXES, split_axis=0, concat_axis=0, tiled=True)  222 us
    all_to_all x4, waiting for transfers between devices, exchange(): lax.all_to_all(parcels, AXES, split_axis=0, concat_axis=0, tiled=True)  86.5 us
    pallas_call x2, Pallas kernels, convolve(): pl.pallas_call(conv_kernel, in_specs=[IN_SMEM, IN_ANY, IN_VMEM, IN_ANY, I...  84.9 us
    pallas_call x1, Pallas kernels, next_send(): pl.pallas_call(next_send_kernel, in_specs=[IN_ANY, IN_SMEM] + [IN_VMEM] *...  15.5 us
    pallas_call x1, Pallas kernels, first_send(): pl.pallas_call(first_send_kernel, in_specs=[IN_ANY, IN_VMEM], out_specs=I...  13.3 us
  transfers between devices with their start and end apart: 4, of which 4 were waited for; matrix products, arithmetic and copies ran while one was open for 2% of the time, Pallas kernels for 2%

profile of v5, /device:TPU:1, one launch (start us, length us, event | category | flops | bytes accessed | tf_op | source)
XLA Modules:
  0.0 451.0 jit_solution(12848016138933968607)
XLA Ops:
  0.0 3.9 copy.9
  3.9 13.3 %first_send.1 = bf16[128,96,128]{2,1,0:T(8,128)(2,1)} custom-call(s32[16,8,128]{2,1,0:T(8,128)} %bitcast.8, bf16[8192,96]{1,0:T(8,128)(2,1)} %bitcast.6), custom_call_target="tpu_custom_call" | custom-call | tf_op jit(solution)/shard_map/first_send/pallas_call | solution.py:264
  17.1 0.0 copy-start.6
  17.2 11.5 %all-to-all-start = ((bf16[128,96,128]{2,1,0:T(8,128)(2,1)}), bf16[128,96,128]{2,1,0:T(8,128)(2,1)S(1)}, u32[]{:S(2)}, u32[]{:S(2)}) async-start(bf16[128,96,128]{2,1,0:T(8,128)(2,1)} %first_send.1), calls=%async_computation | async-start | bytes 6291456 | tf_op jit(solution)/shard_map/all_to_all | solution.py:353
  28.7 0.0 copy-done.6
  28.7 0.6 dynamic_slice.3.live
  29.3 1.4 fusion.middle
  30.7 1.3 pad_slice_fusion.5
  31.9 1.0 pad_maximum_fusion.weight
  32.9 0.0 copy-start.4
  32.9 36.7 %all-to-all-done.parcels = bf16[128,96,128]{2,1,0:T(8,128)(2,1)S(1)} async-done(((bf16[128,96,128]{2,1,0:T(8,128)(2,1)}), bf16[128,96,128]{2,1,0:T(8,128)(2,1)S(1)}, u32[]{:S(2)}, u32[]{:S(2)}) %all-to-all-start) | async-done | bytes 3145760 | tf_op jit(solution)/shard_map/all_to_all | solution.py:353
  69.6 1.7 copy-done
  71.3 42.4 %sparse_conv.2 = (f32[8192,128]{1,0:T(8,128)}, f32[128,2,128]{2,1,0:T(2,128)}) custom-call(s32[1]{0:T(128)} %dynamic_slice.3.live, s32[27,8192]{1,0:T(8,128)} %maps.3, bf16[8192,96]{1,0:T(8,128)(2,1)} %bitcast.7, bf16[128,96,128]{2,1,0:T(8,128)(2,1)} %copy-done, bf16[13,256,128]{2,1,0:T(8,128)(2,1)} %pad_maximum_fusion.weight, bf16[128,128]{1,0:T(8,128)(2,1)} %fusion.middle), custom_call_target="tpu_custom_call" | custom-call | tf_op jit(solution)/shard_map/jit(convolve)/sparse_conv/pallas_call | solution.py:292
  113.7 103.3 %all-to-all-start.1 = ((f32[128,2,128]{2,1,0:T(2,128)}), f32[128,2,128]{2,1,0:T(2,128)S(1)}, u32[]{:S(2)}, u32[]{:S(2)}) async-start(f32[128,2,128]{2,1,0:T(2,128)} %get-tuple-element.12), calls=%async_computation.1 | async-start | bytes 262144 | tf_op jit(solution)/shard_map/all_to_all | solution.py:353
  217.0 0.0 copy-done.4
  217.0 0.0 copy-done.5
  217.0 0.6 pad_slice_fusion.6
  217.6 9.4 %all-to-all-done.1.stats = f32[128,2,128]{2,1,0:T(2,128)S(1)} async-done(((f32[128,2,128]{2,1,0:T(2,128)}), f32[128,2,128]{2,1,0:T(2,128)S(1)}, u32[]{:S(2)}, u32[]{:S(2)}) %all-to-all-start.1) | async-done | bytes 131104 | tf_op jit(solution)/shard_map/all_to_all | solution.py:353
  227.0 0.7 copy-done.2
  227.7 15.5 %next_send.1 = (bf16[128,96,128]{2,1,0:T(8,128)(2,1)}, bf16[8192,96]{1,0:T(8,128)(2,1)}) custom-call(s32[16,8,128]{2,1,0:T(8,128)} %bitcast.9, s32[1]{0:T(128)} %dynamic_slice.3.live, f32[8192,128]{1,0:T(8,128)} %get-tuple-element.11.conved, f32[128,2,128]{2,1,0:T(2,128)} %copy-done.2, f32[1,128]{1,0:T(1,128)} %get-tuple-element.25.gain, ...), custom_call_target="tpu_custom_call" | custom-call | tf_op jit(solution)/shard_map/next_send/pallas_call | solution.py:276
  243.2 4.2 all-to-all-start.2
  247.4 1.4 fusion.1.middle
  248.7 1.3 pad_slice_fusion.2
  250.0 1.0 pad_maximum_fusion.1.weight
  251.0 37.3 %all-to-all-done.2.parcels = bf16[128,96,128]{2,1,0:T(8,128)(2,1)S(1)} async-done(((bf16[128,96,128]{2,1,0:T(8,128)(2,1)}), bf16[128,96,128]{2,1,0:T(8,128)(2,1)S(1)}, u32[]{:S(2)}, u32[]{:S(2)}) %all-to-all-start.2) | async-done | bytes 3145760 | tf_op jit(solution)/shard_map/all_to_all | solution.py:353
  288.3 1.7 copy-done.1
  290.0 42.5 %sparse_conv.3 = (f32[8192,128]{1,0:T(8,128)}, f32[128,2,128]{2,1,0:T(2,128)}) custom-call(s32[1]{0:T(128)} %dynamic_slice.3.live, s32[27,8192]{1,0:T(8,128)} %maps.3, bf16[8192,96]{1,0:T(8,128)(2,1)} %get-tuple-element.13.own, bf16[128,96,128]{2,1,0:T(8,128)(2,1)} %copy-done.1, bf16[13,256,128]{2,1,0:T(8,128)(2,1)} %pad_maximum_fusion.1.weight, ...), custom_call_target="tpu_custom_call" | custom-call | tf_op jit(solution)/shard_map/jit(convolve)/sparse_conv/pallas_call | solution.py:292
  332.5 103.3 %all-to-all-start.3 = ((f32[128,2,128]{2,1,0:T(2,128)}), f32[128,2,128]{2,1,0:T(2,128)S(1)}, u32[]{:S(2)}, u32[]{:S(2)}) async-start(f32[128,2,128]{2,1,0:T(2,128)} %get-tuple-element.16), calls=%async_computation.3 | async-start | bytes 262144 | tf_op jit(solution)/shard_map/all_to_all | solution.py:353
  435.7 7.0 %turn.1.turned = f32[96,8192]{1,0:T(8,128)} custom-call(f32[8192,128]{1,0:T(8,128)} %get-tuple-element.15.conved), custom_call_target="tpu_custom_call" | custom-call | flops 1048576 | bytes 7340032 | tf_op jit(solution)/shard_map/turn/pallas_call | solution.py:318
  442.8 3.0 all-to-all-done.3.stats
  445.8 0.6 copy-done.3
  446.4 4.6 %last_norm.1 = bf16[96,8192]{1,0:T(8,128)(2,1)} custom-call(s32[1]{0:T(128)} %dynamic_slice.3.live, f32[96,8192]{1,0:T(8,128)} %turn.1.turned, f32[128,2,128]{2,1,0:T(2,128)} %copy-done.3, f32[1,128]{1,0:T(1,128)} %get-tuple-element.26.gain, f32[1,128]{1,0:T(1,128)} %get-tuple-element.21.shift), custom_call_target="tpu_custom_call" | custom-call | tf_op jit(solution)/shard_map/last_norm/pallas_call | solution.py:335
  (5 shorter events, 0.0 us)
Async XLA Ops:
  17.1 11.5 %copy-start.6 = (s32[128]{0:T(128)S(1)}, s32[128]{0:T(128)}, u32[]{:S(2)}) copy-start(s32[128]{0:T(128)} %param.11) | copy-start | bytes 1540
  17.2 52.4 %all-to-all-start = ((bf16[128,96,128]{2,1,0:T(8,128)(2,1)}), bf16[128,96,128]{2,1,0:T(8,128)(2,1)S(1)}, u32[]{:S(2)}, u32[]{:S(2)}) async-start(bf16[128,96,128]{2,1,0:T(8,128)(2,1)} %first_send.1), calls=%async_computation | async-start | bytes 6291456 | tf_op jit(solution)/shard_map/all_to_all | solution.py:353
  32.9 184.1 %copy-start.4 = (f32[2,96]{1,0:T(2,128)S(1)}, f32[2,96]{1,0:T(2,128)}, u32[]{:S(2)}) copy-start(f32[2,96]{1,0:T(2,128)} %param.15) | copy-start | bytes 2308
  32.9 184.1 %copy-start.5 = (f32[2,96]{1,0:T(2,128)S(1)}, f32[2,96]{1,0:T(2,128)}, u32[]{:S(2)}) copy-start(f32[2,96]{1,0:T(2,128)} %param.14) | copy-start | bytes 2308
  69.6 1.7 copy-start
  113.7 113.3 %all-to-all-start.1 = ((f32[128,2,128]{2,1,0:T(2,128)}), f32[128,2,128]{2,1,0:T(2,128)S(1)}, u32[]{:S(2)}, u32[]{:S(2)}) async-start(f32[128,2,128]{2,1,0:T(2,128)} %get-tuple-element.12), calls=%async_computation.1 | async-start | bytes 262144 | tf_op jit(solution)/shard_map/all_to_all | solution.py:353
  227.0 0.7 copy-start.2
  243.2 45.1 %all-to-all-start.2 = ((bf16[128,96,128]{2,1,0:T(8,128)(2,1)}), bf16[128,96,128]{2,1,0:T(8,128)(2,1)S(1)}, u32[]{:S(2)}, u32[]{:S(2)}) async-start(bf16[128,96,128]{2,1,0:T(8,128)(2,1)} %get-tuple-element.14), calls=%async_computation.2 | async-start | bytes 6291456 | tf_op jit(solution)/shard_map/all_to_all | solution.py:353
  288.3 1.7 copy-start.1
  332.5 113.3 %all-to-all-start.3 = ((f32[128,2,128]{2,1,0:T(2,128)}), f32[128,2,128]{2,1,0:T(2,128)S(1)}, u32[]{:S(2)}, u32[]{:S(2)}) async-start(f32[128,2,128]{2,1,0:T(2,128)} %get-tuple-element.16), calls=%async_computation.3 | async-start | bytes 262144 | tf_op jit(solution)/shard_map/all_to_all | solution.py:353
  445.8 0.6 copy-start.3
